TPU v7x, 512 devices: a whole 4x8x8 slice. The times are simulated.
512 devices in a mesh: tok: 8 (over z), code: 64 (over x, y, core).
Axes of the slice: x: 4, y: 8, z: 8, core: 2. Of those that a mesh axis runs over, the one named last changes fastest.
Arguments:
- latents: bfloat16 [8192, 1024], P(('tok', 'code')), may hold values from -24 to 24
- w_down: bfloat16 [1024, 256], replicated, may hold values from -0.1875 to 0.1875
- w_up: bfloat16 [256, 1024], replicated, may hold values from -0.375 to 0.375
- codebook: bfloat16 [131072, 256], P('code'), may hold values from -24 to 24
- grad_out: bfloat16 [8192, 1024], P(('tok', 'code')), may hold values from -6 to 6
Outputs:
- quantized: bfloat16 [8192, 1024], P(('tok', 'code'))
- grad_latents: bfloat16 [8192, 1024], P(('tok', 'code'))
- grad_codebook: float32 [131072, 256], P(('code', 'tok'))
All inputs are finite; a program needn't handle non-finite values.
Results may differ from a plain program's by a relative error of at most 0.018.
Values may be sent and summed in bfloat16 or wider, within the bound.
A program may use at most 64 MiB of HBM per device.

v0:
```python
import jax
import jax.numpy as jnp
from jax import lax
from jax.sharding import PartitionSpec as P

logit_scale = 64.0
epsilon = 1e-06


def unit_rows(projected):
    lnorm = jnp.sqrt(jnp.sum(projected * projected, axis=1, keepdims=True) + epsilon)
    return (projected / lnorm, lnorm)


def local(latents, w_down, w_up, codebook, grad_out):
    own_rows = latents.shape[0]
    own_start = lax.axis_index("code") * own_rows
    block_latents = lax.all_gather(latents, "code", axis=0, tiled=True)
    block_proj = jnp.dot(block_latents, w_down, preferred_element_type=jnp.float32)
    block_unit, block_norm = unit_rows(block_proj)
    unit_code_lower = block_unit.astype(jnp.bfloat16)
    unit_own = lax.dynamic_slice_in_dim(block_unit, own_start, own_rows, 0)
    lnorm_own = lax.dynamic_slice_in_dim(block_norm, own_start, own_rows, 0)
    code_f = codebook.astype(jnp.float32)
    cnorm = jnp.sqrt(jnp.sum(code_f * code_f, axis=1, keepdims=True) + epsilon)
    normed = code_f / cnorm
    normalized_lower = normed.astype(jnp.bfloat16)
    logits = logit_scale * jnp.dot(
        unit_code_lower, normalized_lower.T, preferred_element_type=jnp.float32
    )
    expo = jnp.exp(logits)
    denom_part = jnp.sum(expo, axis=1)
    weights = expo.astype(jnp.bfloat16)
    numer = jnp.dot(weights, normalized_lower, preferred_element_type=jnp.float32)
    grad_soft_own = jnp.dot(grad_out, w_up.T, preferred_element_type=jnp.float32)
    denom = lax.psum(denom_part, "code")
    numer_own = lax.psum_scatter(numer, "code", scatter_dimension=0, tiled=True)
    denom_own = lax.dynamic_slice_in_dim(denom, own_start, own_rows, 0)
    soft_own = numer_own / denom_own[:, None]
    inner_own = jnp.sum(grad_soft_own * soft_own, axis=1)
    grad_soft, inner = (
        lax.all_gather(grad_soft_own, "code", axis=0, tiled=True),
        lax.all_gather(inner_own, "code", axis=0, tiled=True),
    )
    quantized = jnp.dot(
        soft_own.astype(jnp.bfloat16), w_up, preferred_element_type=jnp.float32
    ).astype(jnp.bfloat16)
    grad_low = grad_soft.astype(jnp.bfloat16)
    prob = expo / denom[:, None]
    hits = jnp.dot(grad_low, normalized_lower.T, preferred_element_type=jnp.float32)
    logit_gradient = logit_scale * prob * (hits - inner[:, None])
    logit_gradient_lower = logit_gradient.astype(jnp.bfloat16)
    prob_low = prob.astype(jnp.bfloat16)
    code_share = codebook.shape[0] // lax.axis_size("tok")
    leading_piece = jnp.dot(prob_low.T, grad_low, preferred_element_type=jnp.float32)
    grad_normed = lax.psum_scatter(
        (
            leading_piece
            + jnp.dot(logit_gradient_lower.T, unit_code_lower, preferred_element_type=jnp.float32)
        ).astype(jnp.bfloat16),
        "tok",
        scatter_dimension=0,
        tiled=True,
    ).astype(jnp.float32)
    share_start = lax.axis_index("tok") * code_share
    normed_share = lax.dynamic_slice_in_dim(normed, share_start, code_share, 0)
    cnorm_share = lax.dynamic_slice_in_dim(cnorm, share_start, code_share, 0)
    grad_codebook = (
        grad_normed - normed_share * jnp.sum(normed_share * grad_normed, axis=1, keepdims=True)
    ) / cnorm_share
    unit_code_portion = jnp.dot(
        logit_gradient_lower, normalized_lower, preferred_element_type=jnp.float32
    )
    unit_code_gradient = lax.psum_scatter(
        unit_code_portion, "code", scatter_dimension=0, tiled=True
    )
    grad_proj = (
        (
            unit_code_gradient
            - unit_own * jnp.sum(unit_own * unit_code_gradient, axis=1, keepdims=True)
        )
        / lnorm_own
    ).astype(jnp.bfloat16)
    grad_latents = jnp.dot(grad_proj, w_down.T, preferred_element_type=jnp.float32).astype(
        jnp.bfloat16
    )
    return (quantized, grad_latents, grad_codebook)


def solution(mesh):
    return jax.shard_map(
        local,
        mesh=mesh,
        in_specs=(P(("tok", "code"), None), P(), P(), P("code", None), P(("tok", "code"), None)),
        out_specs=(P(("tok", "code"), None), P(("tok", "code"), None), P(("code", "tok"), None)),
        check_vma=False,
    )
```

profile of v0, /device:TPU:1, one launch (start us, length us, event | category | flops | bytes accessed | tf_op | source)
XLA Modules:
  0.0 630.8 jit_solution(6729081866077053597)
XLA Ops:
  7.2 0.0 copy-start
  7.2 0.0 all-gather.2.cloned.1.call-start
  7.2 0.7 all-gather.2.cloned.1.call-update
  7.9 0.0 reduce-scatter.4.cloned.1.call-start
  8.0 1.6 fusion.14
  9.6 0.0 copy-start.1
  9.6 90.2 %all-gather.2.cloned.1.call-done = bf16[1024,1024]{1,0:T(8,128)(2,1)} async-done(((bf16[16,1024]{1,0:T(8,128)(2,1)}), bf16[1024,1024]{1,0:T(8,128)(2,1)}) %all-gather.2.cloned.1.call-update) | async-done | bytes 2097168 | tf_op jit(solution)/shard_map/all_gather | solution.py:18
  99.8 0.0 copy-done
  99.8 2.4 multiply_reduce_fusion
  102.2 0.2 broadcast_divide_fusion
  102.4 0.0 copy-done.1
  102.4 1.8 fusion.1
  104.2 0.0 copy-start.8
  104.2 3.2 copy-done.8
  107.5 0.0 copy-start.2
  107.5 0.0 copy-start.6
  107.5 2.5 fusion.3
  110.0 0.0 reduce-scatter.4.cloned.1.call-update
  110.0 0.0 reduce-scatter.6.cloned.1.call-start
  110.1 1.3 dynamic-slice.8
  112.0 123.7 %psum.7 = f32[1024]{0:T(1024)S(1)} all-reduce(f32[1024]{0:T(1024)S(1)} %get-tuple-element.7), channel_id=1, replica_groups=mesh['tok'=8,'code'=64] {'code'}, use_global_device_ids=true, to_apply=%region_4.0 | all-reduce | flops 1024 | bytes 8192 | tf_op jit(solution)/shard_map/psum | solution.py:36
  235.7 0.1 dynamic_slice.11
  235.8 14.4 %reduce-scatter.4.cloned.1.call-done = f32[16,256]{1,0:T(8,128)} async-done(((f32[1024,256]{1,0:T(8,128)}), f32[16,256]{1,0:T(8,128)}) %reduce-scatter.4.cloned.1.call-update) | async-done | bytes 16400 | tf_op jit(solution)/shard_map/reduce_scatter | solution.py:37
  250.2 0.0 copy-done.2
  250.2 0.0 copy-done.6
  250.2 1.1 fusion.36
  251.3 0.2 dynamic-update-slice
  251.5 129.1 %all-reduce = f32[1024]{0:T(1024)S(1)} all-reduce(f32[1024]{0:T(1024)S(1)} %dynamic-update-slice), channel_id=1, replica_groups=mesh['tok'=8,'code'=64] {'code'}, use_global_device_ids=true, to_apply=%add | all-reduce | flops 1024 | bytes 8192
  380.6 47.5 %all_gather.10 = bf16[1024,256]{1,0:T(8,128)(2,1)S(1)} all-gather(bf16[16,256]{1,0:T(8,128)(2,1)S(1)} %get-tuple-element.3), channel_id=1, replica_groups=mesh['tok'=8,'code'=64] {'code'}, dimensions={0}, use_global_device_ids=true | all-gather | bytes 532480 | tf_op jit(solution)/shard_map/all_gather | solution.py:42
  428.1 0.0 copy-start.3
  428.1 5.1 multiply_convert_fusion
  433.2 0.0 copy-done.3
  433.3 0.0 copy-start.7
  433.3 2.0 copy-done.7
  435.2 2.4 fusion.31
  437.7 0.0 reduce-scatter.6.cloned.1.call-update
  437.7 0.2 reduce-scatter.8.cloned.1.call-start
  437.9 0.0 copy-start.4
  437.9 3.6 fusion.20
  441.5 0.0 copy-done.4
  441.5 6.5 %fusion.11 = bf16[2048,256]{1,0:T(8,128)(2,1)} fusion(f32[2048,256]{1,0:T(8,128)S(1)} %fusion.20, f32[1024,2048]{1,0:T(8,128)} %copy-done.8, f32[1024]{0:T(1024)S(1)} %psum.7, bf16[1024,256]{1,0:T(8,128)(2,1)S(1)} %copy-done.4), kind=kOutput, calls=%fused_computation.12 | convolution fusion | flops 1081081856 | bytes 12062720 | tf_op jit(solution)/shard_map/dot_general | solution.py:55
  448.0 0.0 copy-start.5
  448.0 0.0 reduce-scatter.8.cloned.1.call-update
  448.0 0.1 dynamic-slice.7
  448.1 1.7 convert_divide_fusion
  449.8 0.1 dynamic-slice.6
  449.9 0.0 copy-done.5
  449.9 0.8 convolution_convert_fusion.1
  450.7 126.5 %reduce-scatter.6.cloned.1.call-done = f32[16,256]{1,0:T(8,128)} async-done(((f32[1024,256]{1,0:T(8,128)}), f32[16,256]{1,0:T(8,128)}) %reduce-scatter.6.cloned.1.call-update) | async-done | bytes 16400 | tf_op jit(solution)/shard_map/reduce_scatter | solution.py:74
  577.2 0.8 multiply_reduce_fusion.1
  578.0 1.6 convolution_convert_fusion
  579.6 41.6 %reduce-scatter.8.cloned.1.call-done = bf16[256,256]{1,0:T(8,128)(2,1)} async-done(((bf16[2048,256]{1,0:T(8,128)(2,1)}), bf16[256,256]{1,0:T(8,128)(2,1)}) %reduce-scatter.8.cloned.1.call-update) | async-done | bytes 131088 | tf_op jit(solution)/shard_map/reduce_scatter | solution.py:56
  621.3 1.1 fusion.16
  622.4 1.9 fusion.17
  (3 shorter events, 0.0 us)
Async XLA Ops:
  7.2 92.6 %copy-start = (bf16[1024,256]{1,0:T(8,128)(2,1)S(1)}, bf16[1024,256]{1,0:T(8,128)(2,1)}, u32[]{:S(2)}) copy-start(bf16[1024,256]{1,0:T(8,128)(2,1)} %param.6) | copy-start | bytes 1572868
  7.2 92.6 %all-gather.2.cloned.1.call-start = ((), (), s32[]{:S(2)}) async-start(), calls=%async_computation.3 | async-start | bytes 2129920 | tf_op jit(solution)/shard_map/all_gather | solution.py:18
  7.9 242.3 %reduce-scatter.4.cloned.1.call-start = ((), (), s32[]{:S(2)}) async-start(), calls=%async_computation.4 | async-start | bytes 1064960 | tf_op jit(solution)/shard_map/reduce_scatter | solution.py:37
  9.6 92.9 %copy-start.1 = (bf16[2048,256]{1,0:T(8,128)(2,1)S(1)}, bf16[2048,256]{1,0:T(8,128)(2,1)}, u32[]{:S(2)}) copy-start(bf16[2048,256]{1,0:T(8,128)(2,1)} %param.8) | copy-start | bytes 3145732
  104.2 3.2 copy-start.8
  107.5 142.7 %copy-start.2 = (bf16[256,1024]{1,0:T(8,128)(2,1)S(1)}, bf16[256,1024]{1,0:T(8,128)(2,1)}, u32[]{:S(2)}) copy-start(bf16[256,1024]{1,0:T(8,128)(2,1)} %param.7) | copy-start | bytes 1572868
  107.5 142.7 %copy-start.6 = (bf16[16,1024]{1,0:T(8,128)(2,1)S(1)}, bf16[16,1024]{1,0:T(8,128)(2,1)}, u32[]{:S(2)}) copy-start(bf16[16,1024]{1,0:T(8,128)(2,1)} %param.9) | copy-start | bytes 98308
  110.0 467.2 %reduce-scatter.6.cloned.1.call-start = ((), (), s32[]{:S(2)}) async-start(), calls=%async_computation.5 | async-start | bytes 1064960 | tf_op jit(solution)/shard_map/reduce_scatter | solution.py:74
  428.1 5.1 copy-start.3
  433.3 2.0 copy-start.7
  437.7 183.6 %reduce-scatter.8.cloned.1.call-start = ((), (), s32[]{:S(2)}) async-start(), calls=%async_computation.6 | async-start | bytes 1179648 | tf_op jit(solution)/shard_map/reduce_scatter | solution.py:56
  437.9 3.6 copy-start.4
  448.0 1.9 copy-start.5
Sparse Core Ops, SparseCore 0:
  11.4 88.3 all-gather.1
  110.1 139.9 reduce-scatter.3
  437.8 139.3 reduce-scatter.5
  579.9 41.3 reduce-scatter.7
where the time goes:
time: 635 us; the launch traced here: 631 us
  blocking collectives  300 us (47%)
  waiting for transfers between devices  273 us (43%)
  matrix products  27.8 us (4%)
  between operations  14.6 us (2%)
  other arithmetic  7.33 us (1%)
  local copies, waits for them, and re-layouts  6.97 us (1%)
    unnamed x1, blocking collectives  129 us
    reduce_scatter x1, waiting for transfers between devices, local(): lax.psum_scatter(unit_code_portion, 'code', scatter_dimension=0, tiled=True)  126 us
    psum x1, blocking collectives, local(): denom = lax.psum(denom_part, 'code')  124 us
    all_gather x1, waiting for transfers between devices, local(): block_latents = lax.all_gather(latents, 'code', axis=0, tiled=True)  90.2 us
    all_gather x1, blocking collectives, local(): lax.all_gather(grad_soft_own, 'code', axis=0, tiled=True)  47.5 us
    reduce_scatter x1, waiting for transfers between devices, local(): lax.psum_scatter((leading_piece + jnp.dot(logit_gradient_lower.T, unit_co...  41.6 us
    reduce_scatter x1, waiting for transfers between devices, local(): numer_own = lax.psum_scatter(numer, 'code', scatter_dimension=0, tiled=True)  14.4 us
  transfers between devices with their start and end apart: 4, of which 4 were waited for; matrix products, arithmetic and copies ran while one was open for 3% of the time, Pallas kernels for 0%

commit v1 on v0

v1 whole, which is shorter than its diff:
```python
import functools

import jax
import jax.numpy as jnp
from jax import lax
from jax.experimental import pallas as pl
from jax.experimental.pallas import tpu as pltpu
from jax.sharding import PartitionSpec as P

MESH = pl.DeviceIdType.MESH
F32 = jnp.float32
BF16 = jnp.bfloat16

logit_scale = 64.0
epsilon = 1e-06
X_CHIPS = 4
CORES = 2


def dot_nn(a, b):
    return lax.dot_general(a, b, (((1,), (0,)), ((), ())), preferred_element_type=F32)


def dot_nt(a, b):
    return lax.dot_general(a, b, (((1,), (1,)), ((), ())), preferred_element_type=F32)


def longest(n, sign, half):
    return n // 2 if (sign > 0) == (half == 0) else n // 2 - 1


class RingSum:
    def __init__(self, n, out, into, send_sem, recv_sem, peer):
        self.n, self.out, self.into = n, out, into
        self.send_sem, self.recv_sem, self.peer = send_sem, recv_sem, peer
        self.sent = []

    def copy(self, sign, k, half):
        at = (0 if sign > 0 else 1, k - 1, half)
        return pltpu.make_async_remote_copy(
            src_ref=self.out.at[at],
            dst_ref=self.into.at[at],
            send_sem=self.send_sem.at[at],
            recv_sem=self.recv_sem.at[at],
            device_id=self.peer(sign),
            device_id_type=MESH,
        )

    def arrived(self, sign, k, half):
        self.copy(sign, k, half).wait_recv()
        return self.into[0 if sign > 0 else 1, k - 1, half].astype(F32)

    def send(self, sign, k, half, term):
        top = longest(self.n, sign, half)
        if k > top:
            return
        if k < top:
            term = term + self.arrived(sign, k + 1, half)
        self.out[0 if sign > 0 else 1, k - 1, half] = term.astype(BF16)
        copy = self.copy(sign, k, half)
        copy.start()
        self.sent.append(copy)

    def total(self, half, term):
        for sign in (1, -1):
            if longest(self.n, sign, half) >= 1:
                term = term + self.arrived(sign, 1, half)
        return term


def kernel(
    x_n, y_n, z_n,
    lat_h, wd_h, wu_h, cb_h, go_h,
    q_out, gl_out, gcb_out,
    lat, wd, wu, cb, go, load_sem,
    gat, low, low_t, ee, wt, tr, na, na_in, grad, own,
    ay_s, ay_r, ax_s, ax_r, ah_s, ah_r, as_s, as_r,
    st, st_c_in, st_y_in, st_x_in,
    sc_s, sc_r, sy_s, sy_r, sx_s, sx_r,
    nc_s, nc_r, xo, xi, xo_s, xo_r,
    yo, yi, yo_s, yo_r, fo, fi, fo_s, fo_r,
    zo, zi, zo_s, zo_r,
):
    tok = lax.axis_index("tok")
    code = lax.axis_index("code")
    core = lax.rem(code, CORES)
    y = lax.rem(code // CORES, y_n)
    x = code // (CORES * y_n)
    rows = lat_h.shape[0]
    lat_w = wd_h.shape[1]
    codes = cb_h.shape[0]
    block = y_n * rows
    width = CORES * block
    half_codes = codes // z_n // 2
    half_lat = lat_w // 2

    def at_code(x_at, y_at, core_at):
        return {"code": (x_at * y_n + y_at) * CORES + core_at}

    sibling = at_code(x, y, 1 - core)

    def y_peer(step):
        return at_code(x, lax.rem(y + step, y_n), core)

    def x_peer(step):
        return at_code(lax.rem(x + step + x_n, x_n), y, core)

    def z_peer(step):
        return {"tok": lax.rem(tok + step + z_n, z_n)}

    def remote(src, dst, send_sem, recv_sem, device):
        return pltpu.make_async_remote_copy(
            src_ref=src, dst_ref=dst, send_sem=send_sem, recv_sem=recv_sem, device_id=device, device_id_type=MESH
        )

    sent = []

    def push(*args):
        copy = remote(*args)
        copy.start()
        sent.append(copy)

    def pull(dst, recv_sem, device):
        remote(dst, dst, as_s.at[0], recv_sem, device).wait_recv()

    loads = [
        pltpu.make_async_copy(src, dst, load_sem.at[i])
        for i, (src, dst) in enumerate(((lat_h, lat), (wd_h, wd), (go_h, go), (wu_h, wu), (cb_h, cb)))
    ]
    for load in loads:
        load.start()

    peers = [sibling] + [y_peer(s) for s in range(1, y_n)] + [x_peer(s) for s in range(1, x_n)]
    peers += [z_peer(1), z_peer(-1)]
    barrier = pltpu.get_barrier_semaphore()
    for peer in peers:
        pl.semaphore_signal(barrier, inc=1, device_id=peer, device_id_type=MESH)

    loads[0].wait()
    loads[1].wait()
    proj = dot_nn(lat[...], wd[...])
    lnorm = jnp.sqrt(jnp.sum(proj * proj, axis=1, keepdims=True) + epsilon)
    unit = proj / lnorm
    own[0] = unit
    own[1] = jnp.broadcast_to(lnorm, unit.shape)
    own_rows = pl.ds(pl.multiple_of(core * block + y * rows, rows), rows)
    gat[0, 0, own_rows, :] = (unit.astype(BF16).astype(F32) * logit_scale).astype(BF16)
    loads[2].wait()
    loads[3].wait()
    gat[0, 1, own_rows, :] = dot_nt(go[...], wu[...]).astype(BF16)

    pl.semaphore_wait(barrier, len(peers))

    for s in range(1, y_n):
        piece = gat.at[0, :, own_rows, :]
        push(piece, piece, ay_s.at[s - 1], ay_r.at[s - 1], y_peer(s))

    loads[4].wait()
    step_rows = min(256, codes)

    def normalize(i, _):
        at = pl.ds(pl.multiple_of(i * step_rows, step_rows), step_rows)
        c = cb[at, :].astype(F32)
        n = c / jnp.sqrt(jnp.sum(c * c, axis=1, keepdims=True) + epsilon)
        n = n.astype(BF16)
        low[at, :] = n
        low_t[:, at] = n.T
        return 0

    lax.fori_loop(0, codes // step_rows, normalize, 0)

    my_block = pl.ds(pl.multiple_of(core * block, block), block)
    its_block = pl.ds(pl.multiple_of((1 - core) * block, block), block)
    first_half = pl.ds(pl.multiple_of(core * block, block // 2), block // 2)
    second_half = pl.ds(pl.multiple_of(core * block + block // 2, block // 2), block // 2)

    for s in range(1, y_n):
        from_y = lax.rem(y + y_n - s, y_n)
        at = pl.ds(pl.multiple_of(core * block + from_y * rows, rows), rows)
        pull(gat.at[0, :, at, :], ay_r.at[s - 1], y_peer(s))

    def to_sibling(j):
        piece = gat.at[j, :, my_block, :]
        push(piece, piece, as_s.at[j], as_r.at[j], sibling)

    def from_sibling(j):
        pull(gat.at[j, :, its_block, :], as_r.at[j], sibling)

    mine = gat.at[0, :, my_block, :]
    push(mine, gat.at[x_n - 1, :, my_block, :], ax_s.at[0], ax_r.at[0], x_peer(1))
    push(mine, gat.at[1, :, my_block, :], ax_s.at[1], ax_r.at[1], x_peer(-1))
    to_sibling(0)

    tile = min(512, codes)
    sums = {}

    def forward(j):
        u = gat[j, 0]
        g = gat[j, 1]
        col = pl.ds(j * width, width)
        col_h = pl.ds((x_n + j) * width, width)

        def step(i, carry):
            den, inn = carry
            at = pl.ds(pl.multiple_of(i * tile, tile), tile)
            n = low[at, :]
            e = jnp.exp(dot_nt(n, u))
            eh = e * dot_nt(n, g)
            ee[at, col] = e.astype(BF16)
            ee[at, col_h] = eh.astype(BF16)
            return den + e.reshape(tile // 8, 8, width).sum(0), inn + eh.reshape(tile // 8, 8, width).sum(0)

        zero = jnp.zeros((8, width), F32)
        den, inn = lax.fori_loop(0, codes // tile, step, (zero, zero))
        sums[j] = (jnp.sum(den, axis=0, keepdims=True), jnp.sum(inn, axis=0, keepdims=True))
        tr[j, 0] = u.T
        tr[j, 1] = g.T

    def weighted(j):
        na[j, 0] = dot_nn(low_t[...], ee[:, pl.ds(j * width, width)]).astype(BF16)
        na[j, 1] = dot_nn(low_t[...], ee[:, pl.ds((x_n + j) * width, width)]).astype(BF16)
        push(na.at[j, 1 - core], na_in.at[j], nc_s.at[j], nc_r.at[j], sibling)

    from_sibling(0)
    forward(0)

    pull(gat.at[x_n - 1, :, my_block, :], ax_r.at[0], x_peer(-1))
    push(
        gat.at[x_n - 1, :, first_half, :], gat.at[2, :, first_half, :], ah_s.at[0], ah_r.at[0], x_peer(1)
    )
    to_sibling(x_n - 1)
    pull(gat.at[1, :, my_block, :], ax_r.at[1], x_peer(1))
    push(gat.at[1, :, second_half, :], gat.at[2, :, second_half, :], ah_s.at[1], ah_r.at[1], x_peer(-1))
    to_sibling(1)

    weighted(0)
    from_sibling(x_n - 1)
    forward(x_n - 1)
    from_sibling(1)
    forward(1)
    pull(gat.at[2, :, first_half, :], ah_r.at[0], x_peer(-1))
    pull(gat.at[2, :, second_half, :], ah_r.at[1], x_peer(1))
    to_sibling(2)
    weighted(x_n - 1)
    weighted(1)
    from_sibling(2)
    forward(2)

    line = lax.broadcasted_iota(jnp.int32, (2 * x_n, width), 0)
    part = jnp.zeros((2 * x_n, width), F32)
    for j in range(x_n):
        at_x = lax.rem(x + j, x_n)
        part = jnp.where(line == 2 * at_x, sums[j][0], part)
        part = jnp.where(line == 2 * at_x + 1, sums[j][1], part)
    st[0] = part
    push(st.at[0], st_c_in, sc_s.at[0], sc_r.at[0], sibling)
    weighted(2)
    pull(st_c_in, sc_r.at[0], sibling)
    st[1] = part = part + st_c_in[...]
    for s in range(1, y_n):
        push(st.at[1], st_y_in.at[s - 1], sy_s.at[s - 1], sy_r.at[s - 1], y_peer(s))

    ring_x = RingSum(x_n, xo, xi, xo_s, xo_r, x_peer)

    def paired(j, half):
        at = pl.ds(half * half_lat, half_lat)
        return na[j, core, at, :].astype(F32) + na_in[j, at, :].astype(F32)

    for j in range(x_n):
        pull(na_in.at[j], nc_r.at[j], sibling)

    for s in range(1, y_n):
        pull(st_y_in.at[s - 1], sy_r.at[s - 1], y_peer(s))
        part = part + st_y_in[s - 1]
    st[2] = part
    for s in range(1, x_n):
        push(st.at[2], st_x_in.at[s - 1], sx_s.at[s - 1], sx_r.at[s - 1], x_peer(s))
    for s in range(1, x_n):
        pull(st_x_in.at[s - 1], sx_r.at[s - 1], x_peer(s))
    total = jnp.zeros((2 * x_n, width), F32)
    for at_x in range(x_n):
        term = jnp.where(x == at_x, part, 0.0)
        for s in range(1, x_n):
            term = jnp.where(lax.rem(x + x_n - s, x_n) == at_x, st_x_in[s - 1], term)
        total = total + term

    def line_of(at):
        return jnp.sum(jnp.where(line == at, total, 0.0), axis=0, keepdims=True)

    for j in range(x_n):
        at_x = lax.rem(x + j, x_n)
        den = line_of(2 * at_x)
        inner = line_of(2 * at_x + 1) / den
        inv = 1.0 / den
        ut = tr[j, 0].astype(F32)
        gt = tr[j, 1].astype(F32)
        wt[:, pl.ds(j * width, width)] = ((gt - inner * ut) * inv).astype(BF16)
        wt[:, pl.ds((x_n + j) * width, width)] = (ut * inv).astype(BF16)

    ring_z = RingSum(z_n, zo, zi, zo_s, zo_r, z_peer)
    share = codes // z_n

    def shard(step):
        at = pl.ds(pl.multiple_of(lax.rem(tok + step + z_n, z_n) * share, share), share)
        grad[step % z_n] = dot_nt(ee[at, :], wt[...])

    def send_z(sign, k, half):
        ring_z.send(sign, k, half, grad[(sign * k) % z_n, pl.ds(half * half_codes, half_codes), :])

    def send_x(sign, k, half):
        ring_x.send(sign, k, half, paired((sign * k) % x_n, half))

    top = z_n // 2
    shard(top)
    send_z(1, top, 0)
    send_z(-1, top, 1)
    send_x(1, 2, 0)
    send_x(-1, 2, 1)
    send_x(1, 1, 1)
    send_x(-1, 1, 0)

    done = {top}

    def shards(k):
        if k < 1:
            return
        for sign in (1, -1):
            if (sign * k) % z_n not in done:
                shard(sign * k)
                done.add((sign * k) % z_n)

    def late_x():
        send_x(1, 1, 0)
        send_x(-1, 1, 1)

    def tokens_y():
        for half in range(2):
            both = ring_x.total(half, paired(0, half)).T.astype(BF16)
            for to_core in range(CORES):
                for to_y in range(y_n):
                    first = to_core * block + to_y * rows
                    yo[to_y, to_core * rows : (to_core + 1) * rows, half * half_lat : (half + 1) * half_lat] = both[
                        first : first + rows
                    ]
        for s in range(1, y_n):
            push(yo.at[lax.rem(y + s, y_n)], yi.at[s - 1], yo_s.at[s - 1], yo_r.at[s - 1], y_peer(s))

    def tokens_core():
        chip = yo[y].astype(F32)
        for s in range(1, y_n):
            pull(yi.at[s - 1], yo_r.at[s - 1], y_peer(s))
            chip = chip + yi[s - 1].astype(F32)
        fo[0] = chip[:rows]
        fo[1] = chip[rows:]
        push(fo.at[1 - core], fi, fo_s.at[0], fo_r.at[0], sibling)

    between = {top - 1: late_x, top - 2: tokens_y, top - 3: tokens_core}
    for k in range(top - 1, 0, -1):
        shards(k)
        if k == top - 1:
            send_z(1, k, 1)
            send_z(-1, k, 0)
            shards(k - 1)
            send_z(1, k, 0)
            send_z(-1, k, 1)
        else:
            send_z(1, k, 1)
            send_z(-1, k, 0)
            send_z(1, k, 0)
            send_z(-1, k, 1)
        if k in between:
            between.pop(k)()
    shard(0)
    for k in sorted(between, reverse=True):
        between[k]()

    pull(fi, fo_r.at[0], sibling)
    kept, given = fo[core], fi[...]
    numer = jnp.where(core == 0, kept, given)
    pulled = jnp.where(core == 0, given, kept)
    lane = lax.broadcasted_iota(jnp.int32, (rows, width), 1)
    first = lax.broadcasted_iota(jnp.int32, (rows, width), 0) + (core * block + y * rows)

    def column(at):
        return jnp.sum(jnp.where(lane == first, line_of(at), 0.0), axis=1, keepdims=True)

    den = column(2 * x)
    inner = column(2 * x + 1) / den
    soft = numer / den
    q_out[...] = dot_nn(soft.astype(BF16), wu[...]).astype(BF16)
    grad_unit = (pulled - inner * numer) / den * logit_scale
    unit = own[0]
    grad_proj = (grad_unit - unit * jnp.sum(unit * grad_unit, axis=1, keepdims=True)) / own[1]
    gl_out[...] = dot_nt(grad_proj.astype(BF16), wd[...]).astype(BF16)

    for half in range(2):
        at = pl.ds(half * half_codes, half_codes)
        c = cb[pl.ds(pl.multiple_of(tok * share + half * half_codes, half_codes), half_codes), :].astype(F32)
        cnorm = jnp.sqrt(jnp.sum(c * c, axis=1, keepdims=True) + epsilon)
        n = c / cnorm
        gn = ring_z.total(half, grad[0, at, :])
        gcb_out[at, :] = (gn - n * jnp.sum(n * gn, axis=1, keepdims=True)) / cnorm

    for copy in sent + ring_x.sent + ring_z.sent:
        copy.wait_send()


def solution(mesh):
    z_n = mesh.shape["tok"]
    x_n = X_CHIPS
    y_n = mesh.shape["code"] // (CORES * x_n)

    def local(latents, w_down, w_up, codebook, grad_out):
        rows, d = latents.shape
        lat_w = w_down.shape[1]
        codes = codebook.shape[0]
        width = CORES * y_n * rows
        sem = lambda *shape: pltpu.SemaphoreType.DMA(shape)
        ring = lambda n, r, w: [
            pltpu.VMEM((2, n // 2, 2, r, w), BF16),
            pltpu.VMEM((2, n // 2, 2, r, w), BF16),
            sem(2, n // 2, 2),
            sem(2, n // 2, 2),
        ]
        any_space = pl.BlockSpec(memory_space=pl.ANY)
        vmem = pl.BlockSpec(memory_space=pltpu.VMEM)
        stats = (2 * x_n, width)
        return pl.pallas_call(
            functools.partial(kernel, x_n, y_n, z_n),
            out_shape=(
                jax.ShapeDtypeStruct((rows, d), BF16),
                jax.ShapeDtypeStruct((rows, d), BF16),
                jax.ShapeDtypeStruct((codes // z_n, lat_w), F32),
            ),
            in_specs=[any_space] * 5,
            out_specs=(vmem, vmem, vmem),
            scratch_shapes=[
                pltpu.VMEM(latents.shape, BF16),
                pltpu.VMEM(w_down.shape, BF16),
                pltpu.VMEM(w_up.shape, BF16),
                pltpu.VMEM(codebook.shape, BF16),
                pltpu.VMEM(grad_out.shape, BF16),
                sem(5),
                pltpu.VMEM((x_n, 2, width, lat_w), BF16),
                pltpu.VMEM((codes, lat_w), BF16),
                pltpu.VMEM((lat_w, codes), BF16),
                pltpu.VMEM((codes, 2 * x_n * width), BF16),
                pltpu.VMEM((lat_w, 2 * x_n * width), BF16),
                pltpu.VMEM((x_n, 2, lat_w, width), BF16),
                pltpu.VMEM((x_n, 2, lat_w, width), BF16),
                pltpu.VMEM((x_n, lat_w, width), BF16),
                pltpu.VMEM((z_n, codes // z_n, lat_w), F32),
                pltpu.VMEM((2, rows, lat_w), F32),
                sem(y_n - 1), sem(y_n - 1), sem(2), sem(2), sem(2), sem(2), sem(x_n), sem(x_n),
                pltpu.VMEM((3,) + stats, F32),
                pltpu.VMEM(stats, F32),
                pltpu.VMEM((y_n - 1,) + stats, F32),
                pltpu.VMEM((x_n - 1,) + stats, F32),
                sem(1), sem(1), sem(y_n - 1), sem(y_n - 1), sem(x_n - 1), sem(x_n - 1),
                sem(x_n), sem(x_n),
                *ring(x_n, lat_w // 2, width),
                pltpu.VMEM((y_n, CORES * rows, lat_w), BF16),
                pltpu.VMEM((y_n - 1, CORES * rows, lat_w), BF16),
                sem(y_n - 1), sem(y_n - 1),
                pltpu.VMEM((CORES, rows, lat_w), F32),
                pltpu.VMEM((rows, lat_w), F32),
                sem(1), sem(1),
                *ring(z_n, codes // z_n // 2, lat_w),
            ],
            compiler_params=pltpu.CompilerParams(
                collective_id=0, has_side_effects=True, vmem_limit_bytes=52 * 2**20
            ),
        )(latents, w_down, w_up, codebook, grad_out)

    return jax.shard_map(
        local,
        mesh=mesh,
        in_specs=(P(("tok", "code"), None), P(), P(), P("code", None), P(("tok", "code"), None)),
        out_specs=(P(("tok", "code"), None), P(("tok", "code"), None), P(("code", "tok"), None)),
        check_vma=False,
    )
```

time: 635 us -> 65.8 us (0.10)
  blocking collectives: 300 us -> 0 us
  waiting for transfers between devices: 273 us -> 0 us
  Pallas kernels: 0 us -> 59.3 us
  matrix products: 27.8 us -> 0 us
  between operations: 14.6 us -> 0.65 us
  other arithmetic: 7.33 us -> 0 us
    reduce_scatter x3 -> x0, waiting for transfers between devices: 183 us -> none  [the longest x1 126 us: local(): lax.psum_scatter(unit_code_portion, 'code', scatter_dimension=0, tiled=True)]
    unnamed x1 -> x0, blocking collectives: 129 us -> none
    psum x1 -> x0, blocking collectives: 124 us -> none  [local(): denom = lax.psum(denom_part, 'code')]
    all_gather x1 -> x0, waiting for transfers between devices: 90.2 us -> none  [local(): block_latents = lax.all_gather(latents, 'code', axis=0, tiled=True)]
    pallas_call x0 -> x1, Pallas kernels: none -> 59.3 us  [local(): pl.pallas_call(functools.partial(kernel, x_n, y_n, z_n), out_shape=(jax.S...]
    all_gather x1 -> x0, blocking collectives: 47.5 us -> none  [local(): lax.all_gather(grad_soft_own, 'code', axis=0, tiled=True)]
    dot_general x10 -> x0, matrix products: 27.8 us -> none  [the longest x1 6.49 us: local(): jnp.dot(prob_low.T, grad_low, preferred_element_type=jnp.float32)]
  transfers between devices with their start and end apart: 4 -> 0, of which waited for: 4 -> 0; matrix products, arithmetic and copies ran while one was open for 3% -> 0% of each run, Pallas kernels for 0% -> 0%
where the time goes in v1:
time: 65.8 us; the launch traced here: 65.4 us
  Pallas kernels  59.3 us (90%)
  local copies, waits for them, and re-layouts  5.52 us (8%)
    pallas_call x1, Pallas kernels, local(): pl.pallas_call(functools.partial(kernel, x_n, y_n, z_n), out_shape=(jax.S...  59.3 us
    unnamed x11, local copies, waits for them, and re-layouts  5.52 us

profile of v1, /device:TPU:1, one launch (start us, length us, event | category | flops | bytes accessed | tf_op | source)
XLA Modules:
  0.0 65.4 jit_solution(15000776252428478078)
XLA Ops:
  0.6 0.0 copy-start
  0.6 1.0 %copy-done = bf16[1024,256]{1,0:T(8,128)(2,1)S(1)} copy-done((bf16[1024,256]{1,0:T(8,128)(2,1)S(1)}, bf16[1024,256]{1,0:T(8,128)(2,1)}, u32[]{:S(2)}) %copy-start) | copy-done | bytes 524312
  1.7 0.0 copy-start.1
  1.7 1.0 %copy-done.1 = bf16[256,1024]{1,0:T(8,128)(2,1)S(1)} copy-done((bf16[256,1024]{1,0:T(8,128)(2,1)S(1)}, bf16[256,1024]{1,0:T(8,128)(2,1)}, u32[]{:S(2)}) %copy-start.1) | copy-done | bytes 524312
  2.7 0.0 copy-start.2
  2.7 0.8 %copy-done.2 = bf16[16,1024]{1,0:T(8,128)(2,1)S(1)} copy-done((bf16[16,1024]{1,0:T(8,128)(2,1)S(1)}, bf16[16,1024]{1,0:T(8,128)(2,1)}, u32[]{:S(2)}) %copy-start.2) | copy-done | bytes 32792
  3.5 0.0 copy-start.3
  3.5 0.8 %copy-done.3 = bf16[16,1024]{1,0:T(8,128)(2,1)S(1)} copy-done((bf16[16,1024]{1,0:T(8,128)(2,1)S(1)}, bf16[16,1024]{1,0:T(8,128)(2,1)}, u32[]{:S(2)}) %copy-start.3) | copy-done | bytes 32792
  4.2 59.3 %shard_map.76 = (bf16[16,1024]{1,0:T(8,128)(2,1)S(1)}, bf16[16,1024]{1,0:T(8,128)(2,1)S(1)}, f32[256,256]{1,0:T(8,128)S(1)}) custom-call(bf16[16,1024]{1,0:T(8,128)(2,1)S(1)} %copy-done.2, bf16[1024,256]{1,0:T(8,128)(2,1)S(1)} %copy-done, bf16[256,1024]{1,0:T(8,128)(2,1)S(1)} %copy-done.1, bf16[2048,256]{1,0:T(8,128)(2,1)} %cb_h.1, ...), custom_call_target="tpu_custom_call" | custom-call | tf_op jit(solution)/shard_map/pallas_call | solution.py:428
  63.5 0.6 copy.11
  64.1 0.6 copy.12
  64.7 0.7 %copy.13 = f32[256,256]{1,0:T(8,128)} copy(f32[256,256]{1,0:T(8,128)S(1)} %get-tuple-element.8) | data formatting | bytes 524288
Async XLA Ops:
  0.6 1.0 %copy-start = (bf16[1024,256]{1,0:T(8,128)(2,1)S(1)}, bf16[1024,256]{1,0:T(8,128)(2,1)}, u32[]{:S(2)}) copy-start(bf16[1024,256]{1,0:T(8,128)(2,1)} %wd_h.1) | copy-start | bytes 1572868
  1.7 1.0 %copy-start.1 = (bf16[256,1024]{1,0:T(8,128)(2,1)S(1)}, bf16[256,1024]{1,0:T(8,128)(2,1)}, u32[]{:S(2)}) copy-start(bf16[256,1024]{1,0:T(8,128)(2,1)} %wu_h.1) | copy-start | bytes 1572868
  2.7 0.8 %copy-start.2 = (bf16[16,1024]{1,0:T(8,128)(2,1)S(1)}, bf16[16,1024]{1,0:T(8,128)(2,1)}, u32[]{:S(2)}) copy-start(bf16[16,1024]{1,0:T(8,128)(2,1)} %lat_h.1) | copy-start | bytes 98308
  3.5 0.8 %copy-start.3 = (bf16[16,1024]{1,0:T(8,128)(2,1)S(1)}, bf16[16,1024]{1,0:T(8,128)(2,1)}, u32[]{:S(2)}) copy-start(bf16[16,1024]{1,0:T(8,128)(2,1)} %go_h.1) | copy-start | bytes 98308

commit v2 on v1

--- a/solution.py
+++ b/solution.py
@@ -1,4 +1,5 @@
 import functools
+import itertools
 
 import jax
 import jax.numpy as jnp
@@ -25,18 +26,26 @@
     return lax.dot_general(a, b, (((1,), (1,)), ((), ())), preferred_element_type=F32)
 
 
-def longest(n, sign, half):
-    return n // 2 if (sign > 0) == (half == 0) else n // 2 - 1
+def longest(n, parts, sign, part):
+    return n // 2 if (sign > 0) == (part < parts // 2) else n // 2 - 1
 
 
 class RingSum:
     def __init__(self, n, out, into, send_sem, recv_sem, peer):
         self.n, self.out, self.into = n, out, into
+        self.parts = out.shape[2]
         self.send_sem, self.recv_sem, self.peer = send_sem, recv_sem, peer
         self.sent = []
 
-    def copy(self, sign, k, half):
-        at = (0 if sign > 0 else 1, k - 1, half)
+    def order(self, sign):
+        listed = []
+        for k in range(self.n // 2, 0, -1):
+            parts = sorted(range(self.parts), key=lambda p: (longest(self.n, self.parts, sign, p), p))
+            listed += [(k, p) for p in parts if k <= longest(self.n, self.parts, sign, p)]
+        return listed
+
+    def copy(self, sign, k, part):
+        at = (0 if sign > 0 else 1, k - 1, part)
         return pltpu.make_async_remote_copy(
             src_ref=self.out.at[at],
             dst_ref=self.into.at[at],
@@ -46,25 +55,22 @@
             device_id_type=MESH,
         )
 
-    def arrived(self, sign, k, half):
-        self.copy(sign, k, half).wait_recv()
-        return self.into[0 if sign > 0 else 1, k - 1, half].astype(F32)
-
-    def send(self, sign, k, half, term):
-        top = longest(self.n, sign, half)
-        if k > top:
-            return
-        if k < top:
-            term = term + self.arrived(sign, k + 1, half)
-        self.out[0 if sign > 0 else 1, k - 1, half] = term.astype(BF16)
-        copy = self.copy(sign, k, half)
+    def arrived(self, sign, k, part):
+        self.copy(sign, k, part).wait_recv()
+        return self.into[0 if sign > 0 else 1, k - 1, part].astype(F32)
+
+    def send(self, sign, k, part, term):
+        if k < longest(self.n, self.parts, sign, part):
+            term = term + self.arrived(sign, k + 1, part)
+        self.out[0 if sign > 0 else 1, k - 1, part] = term.astype(BF16)
+        copy = self.copy(sign, k, part)
         copy.start()
         self.sent.append(copy)
 
-    def total(self, half, term):
+    def total(self, part, term):
         for sign in (1, -1):
-            if longest(self.n, sign, half) >= 1:
-                term = term + self.arrived(sign, 1, half)
+            if longest(self.n, self.parts, sign, part) >= 1:
+                term = term + self.arrived(sign, 1, part)
         return term
 
 
@@ -74,7 +80,7 @@
     q_out, gl_out, gcb_out,
     lat, wd, wu, cb, go, load_sem,
     gat, low, low_t, ee, wt, tr, na, na_in, grad, own,
-    ay_s, ay_r, ax_s, ax_r, ah_s, ah_r, as_s, as_r,
+    ay_s, ay_r, ax_s, ax_r, as_s, as_r,
     st, st_c_in, st_y_in, st_x_in,
     sc_s, sc_r, sy_s, sy_r, sx_s, sx_r,
     nc_s, nc_r, xo, xi, xo_s, xo_r,
@@ -91,8 +97,10 @@
     codes = cb_h.shape[0]
     block = y_n * rows
     width = CORES * block
-    half_codes = codes // z_n // 2
-    half_lat = lat_w // 2
+    z_parts = zo.shape[2]
+    x_parts = xo.shape[2]
+    z_rows = codes // z_n // z_parts
+    x_rows = lat_w // x_parts
 
     def at_code(x_at, y_at, core_at):
         return {"code": (x_at * y_n + y_at) * CORES + core_at}
@@ -151,33 +159,51 @@
 
     pl.semaphore_wait(barrier, len(peers))
 
-    for s in range(1, y_n):
+    near = sorted(range(1, y_n), key=lambda s: min(s, y_n - s))
+
+    def along_x(s):
+        from_y = lax.rem(y + y_n - s, y_n)
+        at = pl.ds(pl.multiple_of(core * block + from_y * rows, rows), rows)
+        for i, step in enumerate((2, 1, -1)):
+            slot = -step % x_n
+            push(gat.at[0, :, at, :], gat.at[slot, :, at, :], ax_s.at[s, i], ax_r.at[slot - 1], x_peer(step))
+
+    for s in reversed(near):
         piece = gat.at[0, :, own_rows, :]
         push(piece, piece, ay_s.at[s - 1], ay_r.at[s - 1], y_peer(s))
-
-    loads[4].wait()
+    along_x(0)
+
     step_rows = min(256, codes)
-
-    def normalize(i, _):
-        at = pl.ds(pl.multiple_of(i * step_rows, step_rows), step_rows)
+    steps = codes // step_rows
+
+    def normalize(i):
+        at = pl.ds(i * step_rows, step_rows)
         c = cb[at, :].astype(F32)
         n = c / jnp.sqrt(jnp.sum(c * c, axis=1, keepdims=True) + epsilon)
         n = n.astype(BF16)
         low[at, :] = n
         low_t[:, at] = n.T
-        return 0
-
-    lax.fori_loop(0, codes // step_rows, normalize, 0)
+
+    loads[4].wait()
+    ready = 0
+    while ready < steps // 2:
+        normalize(ready)
+        ready += 1
 
     my_block = pl.ds(pl.multiple_of(core * block, block), block)
     its_block = pl.ds(pl.multiple_of((1 - core) * block, block), block)
-    first_half = pl.ds(pl.multiple_of(core * block, block // 2), block // 2)
-    second_half = pl.ds(pl.multiple_of(core * block + block // 2, block // 2), block // 2)
-
-    for s in range(1, y_n):
+
+    for s in near:
         from_y = lax.rem(y + y_n - s, y_n)
         at = pl.ds(pl.multiple_of(core * block + from_y * rows, rows), rows)
         pull(gat.at[0, :, at, :], ay_r.at[s - 1], y_peer(s))
+        along_x(s)
+        if ready < steps:
+            normalize(ready)
+            ready += 1
+    while ready < steps:
+        normalize(ready)
+        ready += 1
 
     def to_sibling(j):
         piece = gat.at[j, :, my_block, :]
@@ -186,9 +212,6 @@
     def from_sibling(j):
         pull(gat.at[j, :, its_block, :], as_r.at[j], sibling)
 
-    mine = gat.at[0, :, my_block, :]
-    push(mine, gat.at[x_n - 1, :, my_block, :], ax_s.at[0], ax_r.at[0], x_peer(1))
-    push(mine, gat.at[1, :, my_block, :], ax_s.at[1], ax_r.at[1], x_peer(-1))
     to_sibling(0)
 
     tile = min(512, codes)
@@ -211,7 +234,7 @@
             return den + e.reshape(tile // 8, 8, width).sum(0), inn + eh.reshape(tile // 8, 8, width).sum(0)
 
         zero = jnp.zeros((8, width), F32)
-        den, inn = lax.fori_loop(0, codes // tile, step, (zero, zero))
+        den, inn = lax.fori_loop(0, codes // tile, step, (zero, zero), unroll=True)
         sums[j] = (jnp.sum(den, axis=0, keepdims=True), jnp.sum(inn, axis=0, keepdims=True))
         tr[j, 0] = u.T
         tr[j, 1] = g.T
@@ -221,28 +244,21 @@
         na[j, 1] = dot_nn(low_t[...], ee[:, pl.ds((x_n + j) * width, width)]).astype(BF16)
         push(na.at[j, 1 - core], na_in.at[j], nc_s.at[j], nc_r.at[j], sibling)
 
+    def from_x(j):
+        pull(gat.at[j, :, my_block, :], ax_r.at[j - 1], x_peer(j))
+        to_sibling(j)
+
     from_sibling(0)
     forward(0)
-
-    pull(gat.at[x_n - 1, :, my_block, :], ax_r.at[0], x_peer(-1))
-    push(
-        gat.at[x_n - 1, :, first_half, :], gat.at[2, :, first_half, :], ah_s.at[0], ah_r.at[0], x_peer(1)
-    )
-    to_sibling(x_n - 1)
-    pull(gat.at[1, :, my_block, :], ax_r.at[1], x_peer(1))
-    push(gat.at[1, :, second_half, :], gat.at[2, :, second_half, :], ah_s.at[1], ah_r.at[1], x_peer(-1))
-    to_sibling(1)
-
+    from_x(x_n - 1)
+    from_x(1)
     weighted(0)
     from_sibling(x_n - 1)
     forward(x_n - 1)
+    from_x(2)
     from_sibling(1)
     forward(1)
-    pull(gat.at[2, :, first_half, :], ah_r.at[0], x_peer(-1))
-    pull(gat.at[2, :, second_half, :], ah_r.at[1], x_peer(1))
-    to_sibling(2)
     weighted(x_n - 1)
-    weighted(1)
     from_sibling(2)
     forward(2)
 
@@ -254,20 +270,28 @@
         part = jnp.where(line == 2 * at_x + 1, sums[j][1], part)
     st[0] = part
     push(st.at[0], st_c_in, sc_s.at[0], sc_r.at[0], sibling)
+    weighted(1)
     weighted(2)
     pull(st_c_in, sc_r.at[0], sibling)
     st[1] = part = part + st_c_in[...]
-    for s in range(1, y_n):
+    for s in reversed(near):
         push(st.at[1], st_y_in.at[s - 1], sy_s.at[s - 1], sy_r.at[s - 1], y_peer(s))
 
     ring_x = RingSum(x_n, xo, xi, xo_s, xo_r, x_peer)
 
-    def paired(j, half):
-        at = pl.ds(half * half_lat, half_lat)
+    def paired(j, part):
+        at = pl.ds(part * x_rows, x_rows)
         return na[j, core, at, :].astype(F32) + na_in[j, at, :].astype(F32)
+
+    def send_x(wanted):
+        for sign in (1, -1):
+            for k, part in ring_x.order(sign):
+                if wanted(k == longest(x_n, x_parts, sign, part)):
+                    ring_x.send(sign, k, part, paired((sign * k) % x_n, part))
 
     for j in range(x_n):
         pull(na_in.at[j], nc_r.at[j], sibling)
+    send_x(lambda begins: begins)
 
     for s in range(1, y_n):
         pull(st_y_in.at[s - 1], sy_r.at[s - 1], y_peer(s))
@@ -275,6 +299,7 @@
     st[2] = part
     for s in range(1, x_n):
         push(st.at[2], st_x_in.at[s - 1], sx_s.at[s - 1], sx_r.at[s - 1], x_peer(s))
+    send_x(lambda begins: not begins)
     for s in range(1, x_n):
         pull(st_x_in.at[s - 1], sx_r.at[s - 1], x_peer(s))
     total = jnp.zeros((2 * x_n, width), F32)
@@ -304,42 +329,16 @@
         at = pl.ds(pl.multiple_of(lax.rem(tok + step + z_n, z_n) * share, share), share)
         grad[step % z_n] = dot_nt(ee[at, :], wt[...])
 
-    def send_z(sign, k, half):
-        ring_z.send(sign, k, half, grad[(sign * k) % z_n, pl.ds(half * half_codes, half_codes), :])
-
-    def send_x(sign, k, half):
-        ring_x.send(sign, k, half, paired((sign * k) % x_n, half))
-
-    top = z_n // 2
-    shard(top)
-    send_z(1, top, 0)
-    send_z(-1, top, 1)
-    send_x(1, 2, 0)
-    send_x(-1, 2, 1)
-    send_x(1, 1, 1)
-    send_x(-1, 1, 0)
-
-    done = {top}
-
-    def shards(k):
-        if k < 1:
-            return
-        for sign in (1, -1):
-            if (sign * k) % z_n not in done:
-                shard(sign * k)
-                done.add((sign * k) % z_n)
-
-    def late_x():
-        send_x(1, 1, 0)
-        send_x(-1, 1, 1)
+    def send_z(sign, k, part):
+        ring_z.send(sign, k, part, grad[(sign * k) % z_n, pl.ds(part * z_rows, z_rows), :])
 
     def tokens_y():
-        for half in range(2):
-            both = ring_x.total(half, paired(0, half)).T.astype(BF16)
+        for part in range(x_parts):
+            both = ring_x.total(part, paired(0, part)).T.astype(BF16)
             for to_core in range(CORES):
                 for to_y in range(y_n):
                     first = to_core * block + to_y * rows
-                    yo[to_y, to_core * rows : (to_core + 1) * rows, half * half_lat : (half + 1) * half_lat] = both[
+                    yo[to_y, to_core * rows : (to_core + 1) * rows, part * x_rows : (part + 1) * x_rows] = both[
                         first : first + rows
                     ]
         for s in range(1, y_n):
@@ -354,25 +353,26 @@
         fo[1] = chip[rows:]
         push(fo.at[1 - core], fi, fo_s.at[0], fo_r.at[0], sibling)
 
-    between = {top - 1: late_x, top - 2: tokens_y, top - 3: tokens_core}
-    for k in range(top - 1, 0, -1):
-        shards(k)
-        if k == top - 1:
-            send_z(1, k, 1)
-            send_z(-1, k, 0)
-            shards(k - 1)
-            send_z(1, k, 0)
-            send_z(-1, k, 1)
-        else:
-            send_z(1, k, 1)
-            send_z(-1, k, 0)
-            send_z(1, k, 0)
-            send_z(-1, k, 1)
-        if k in between:
-            between.pop(k)()
+    top = z_n // 2
+    shard(top)
+    computed = {top}
+    after = {top: lambda: None, top - 1: tokens_y, top - 2: tokens_core}
+    for k in range(top, 0, -1):
+        messages = {sign: [m for m in ring_z.order(sign) if m[0] == k] for sign in (1, -1)}
+        ahead = [(sign * k) % z_n for sign in (1, -1)]
+        for step in ahead:
+            if step not in computed:
+                shard(step)
+                computed.add(step)
+        for pair in itertools.zip_longest(messages[1], messages[-1]):
+            for sign, message in zip((1, -1), pair):
+                if message is not None:
+                    send_z(sign, *message)
+        if k in after:
+            after.pop(k)()
     shard(0)
-    for k in sorted(between, reverse=True):
-        between[k]()
+    for k in sorted(after, reverse=True):
+        after[k]()
 
     pull(fi, fo_r.at[0], sibling)
     kept, given = fo[core], fi[...]
@@ -393,16 +393,25 @@
     grad_proj = (grad_unit - unit * jnp.sum(unit * grad_unit, axis=1, keepdims=True)) / own[1]
     gl_out[...] = dot_nt(grad_proj.astype(BF16), wd[...]).astype(BF16)
 
-    for half in range(2):
-        at = pl.ds(half * half_codes, half_codes)
-        c = cb[pl.ds(pl.multiple_of(tok * share + half * half_codes, half_codes), half_codes), :].astype(F32)
+    for part in sorted(range(z_parts), key=lambda p: min(p, z_parts - 1 - p), reverse=True):
+        at = pl.ds(part * z_rows, z_rows)
+        c = cb[pl.ds(pl.multiple_of(tok * share + part * z_rows, z_rows), z_rows), :].astype(F32)
         cnorm = jnp.sqrt(jnp.sum(c * c, axis=1, keepdims=True) + epsilon)
         n = c / cnorm
-        gn = ring_z.total(half, grad[0, at, :])
+        gn = ring_z.total(part, grad[0, at, :])
         gcb_out[at, :] = (gn - n * jnp.sum(n * gn, axis=1, keepdims=True)) / cnorm
 
     for copy in sent + ring_x.sent + ring_z.sent:
         copy.wait_send()
+
+
+def place(*refs):
+    n = len(refs) // 2
+    copies = [pltpu.make_async_copy(refs[i], refs[n + i], refs[-1].at[i]) for i in range(n)]
+    for copy in copies:
+        copy.start()
+    for copy in copies:
+        copy.wait()
 
 
 def solution(mesh):
@@ -416,22 +425,23 @@
         codes = codebook.shape[0]
         width = CORES * y_n * rows
         sem = lambda *shape: pltpu.SemaphoreType.DMA(shape)
-        ring = lambda n, r, w: [
-            pltpu.VMEM((2, n // 2, 2, r, w), BF16),
-            pltpu.VMEM((2, n // 2, 2, r, w), BF16),
-            sem(2, n // 2, 2),
-            sem(2, n // 2, 2),
+        ring = lambda n, parts, r, w: [
+            pltpu.VMEM((2, n // 2, parts, r // parts, w), BF16),
+            pltpu.VMEM((2, n // 2, parts, r // parts, w), BF16),
+            sem(2, n // 2, parts),
+            sem(2, n // 2, parts),
         ]
         any_space = pl.BlockSpec(memory_space=pl.ANY)
         vmem = pl.BlockSpec(memory_space=pltpu.VMEM)
         stats = (2 * x_n, width)
-        return pl.pallas_call(
+        outs = (
+            jax.ShapeDtypeStruct((rows, d), BF16),
+            jax.ShapeDtypeStruct((rows, d), BF16),
+            jax.ShapeDtypeStruct((codes // z_n, lat_w), F32),
+        )
+        results = pl.pallas_call(
             functools.partial(kernel, x_n, y_n, z_n),
-            out_shape=(
-                jax.ShapeDtypeStruct((rows, d), BF16),
-                jax.ShapeDtypeStruct((rows, d), BF16),
-                jax.ShapeDtypeStruct((codes // z_n, lat_w), F32),
-            ),
+            out_shape=outs,
             in_specs=[any_space] * 5,
             out_specs=(vmem, vmem, vmem),
             scratch_shapes=[
@@ -451,26 +461,33 @@
                 pltpu.VMEM((x_n, lat_w, width), BF16),
                 pltpu.VMEM((z_n, codes // z_n, lat_w), F32),
                 pltpu.VMEM((2, rows, lat_w), F32),
-                sem(y_n - 1), sem(y_n - 1), sem(2), sem(2), sem(2), sem(2), sem(x_n), sem(x_n),
+                sem(y_n - 1), sem(y_n - 1), sem(y_n, x_n - 1), sem(x_n - 1), sem(x_n), sem(x_n),
                 pltpu.VMEM((3,) + stats, F32),
                 pltpu.VMEM(stats, F32),
                 pltpu.VMEM((y_n - 1,) + stats, F32),
                 pltpu.VMEM((x_n - 1,) + stats, F32),
                 sem(1), sem(1), sem(y_n - 1), sem(y_n - 1), sem(x_n - 1), sem(x_n - 1),
                 sem(x_n), sem(x_n),
-                *ring(x_n, lat_w // 2, width),
+                *ring(x_n, 2, lat_w, width),
                 pltpu.VMEM((y_n, CORES * rows, lat_w), BF16),
                 pltpu.VMEM((y_n - 1, CORES * rows, lat_w), BF16),
                 sem(y_n - 1), sem(y_n - 1),
                 pltpu.VMEM((CORES, rows, lat_w), F32),
                 pltpu.VMEM((rows, lat_w), F32),
                 sem(1), sem(1),
-                *ring(z_n, codes // z_n // 2, lat_w),
+                *ring(z_n, 4, codes // z_n, lat_w),
             ],
             compiler_params=pltpu.CompilerParams(
-                collective_id=0, has_side_effects=True, vmem_limit_bytes=52 * 2**20
+                collective_id=0, has_side_effects=True, vmem_limit_bytes=64 * 2**20 - 64 * 2**10
             ),
         )(latents, w_down, w_up, codebook, grad_out)
+        return pl.pallas_call(
+            place,
+            out_shape=outs,
+            in_specs=[vmem] * 3,
+            out_specs=(any_space,) * 3,
+            scratch_shapes=[sem(3)],
+        )(*results)
 
     return jax.shard_map(
         local,

time: 65.8 us -> 58.3 us (0.89)
  local copies, waits for them, and re-layouts: 5.52 us -> 0 us
  Pallas kernels: 59.3 us -> 56.7 us
    unnamed x11 -> x0, local copies, waits for them, and re-layouts: 5.52 us -> none
    pallas_call x1 -> x2, Pallas kernels: 59.3 us -> 56.7 us  [the longest x1 54.9 us: local(): pl.pallas_call(functools.partial(kernel, x_n, y_n, z_n), out_shape=outs,...]
where the time goes in v2:
time: 58.3 us; the launch traced here: 57.3 us
  Pallas kernels  56.7 us (97%)
  between operations  0.64 us (1%)
    pallas_call x1, Pallas kernels, local(): pl.pallas_call(functools.partial(kernel, x_n, y_n, z_n), out_shape=outs,...  54.9 us
    pallas_call x1, Pallas kernels, local(): pl.pallas_call(place, out_shape=outs, in_specs=[vmem] * 3, out_specs=(any...  1.74 us

profile of v2, /device:TPU:1, one launch (start us, length us, event | category | flops | bytes accessed | tf_op | source)
XLA Modules:
  0.0 57.3 jit_solution(2860690057610155436)
XLA Ops:
  0.6 54.9 %shard_map.76 = (bf16[16,1024]{1,0:T(8,128)(2,1)}, bf16[16,1024]{1,0:T(8,128)(2,1)}, f32[256,256]{1,0:T(8,128)}) custom-call(bf16[16,1024]{1,0:T(8,128)(2,1)} %lat_h.1, bf16[1024,256]{1,0:T(8,128)(2,1)} %wd_h.1, bf16[256,1024]{1,0:T(8,128)(2,1)} %wu_h.1, bf16[2048,256]{1,0:T(8,128)(2,1)} %cb_h.1, bf16[16,1024]{1,0:T(8,128)(2,1)} %go_h.1), custom_call_target="tpu_custom_call" | custom-call | tf_op jit(solution)/shard_map/pallas_call | solution.py:442
  55.6 1.7 %shard_map.77 = (bf16[16,1024]{1,0:T(8,128)(2,1)}, bf16[16,1024]{1,0:T(8,128)(2,1)}, f32[256,256]{1,0:T(8,128)}) custom-call(bf16[16,1024]{1,0:T(8,128)(2,1)} %get-tuple-element.6.refs_0_, bf16[16,1024]{1,0:T(8,128)(2,1)} %get-tuple-element.7.refs_1_, f32[256,256]{1,0:T(8,128)} %get-tuple-element.8.refs_2_), custom_call_target="tpu_custom_call" | custom-call | tf_op jit(solution)/shard_map/pallas_call | solution.py:484

commit v3 on v2

v3 whole, which is shorter than its diff:
```python
import functools
import itertools

import jax
import jax.numpy as jnp
from jax import lax
from jax.experimental import pallas as pl
from jax.experimental.pallas import tpu as pltpu
from jax.sharding import PartitionSpec as P

MESH = pl.DeviceIdType.MESH
F32 = jnp.float32
BF16 = jnp.bfloat16

logit_scale = 64.0
epsilon = 1e-06
X_CHIPS = 4
CORES = 2


def dot_nn(a, b):
    return lax.dot_general(a, b, (((1,), (0,)), ((), ())), preferred_element_type=F32)


def dot_nt(a, b):
    return lax.dot_general(a, b, (((1,), (1,)), ((), ())), preferred_element_type=F32)


def longest(n, parts, sign, part):
    return n // 2 if (sign > 0) == (part < parts // 2) else n // 2 - 1


class RingSum:
    def __init__(self, n, out, into, send_sem, recv_sem, peer):
        self.n, self.out, self.into = n, out, into
        self.parts = out.shape[2]
        self.send_sem, self.recv_sem, self.peer = send_sem, recv_sem, peer
        self.sent = []

    def order(self, sign):
        listed = []
        for k in range(self.n // 2, 0, -1):
            parts = sorted(range(self.parts), key=lambda p: (longest(self.n, self.parts, sign, p), p))
            listed += [(k, p) for p in parts if k <= longest(self.n, self.parts, sign, p)]
        return listed

    def copy(self, sign, k, part):
        at = (0 if sign > 0 else 1, k - 1, part)
        return pltpu.make_async_remote_copy(
            src_ref=self.out.at[at],
            dst_ref=self.into.at[at],
            send_sem=self.send_sem.at[at],
            recv_sem=self.recv_sem.at[at],
            device_id=self.peer(sign),
            device_id_type=MESH,
        )

    def arrived(self, sign, k, part):
        self.copy(sign, k, part).wait_recv()
        return self.into[0 if sign > 0 else 1, k - 1, part].astype(F32)

    def send(self, sign, k, part, term):
        if k < longest(self.n, self.parts, sign, part):
            term = term + self.arrived(sign, k + 1, part)
        self.out[0 if sign > 0 else 1, k - 1, part] = term.astype(BF16)
        copy = self.copy(sign, k, part)
        copy.start()
        self.sent.append(copy)

    def total(self, part, term):
        for sign in (1, -1):
            if longest(self.n, self.parts, sign, part) >= 1:
                term = term + self.arrived(sign, 1, part)
        return term


def kernel(
    x_n, y_n, z_n,
    lat_h, wd_h, wu_h, cb_h, go_h,
    q_out, gl_out, gcb_out,
    lat, wd, wu, cb, go, load_sem, cb_s, cb_r,
    gat, low, low_t, ee, wt, tr, na, grad, own,
    ay_s, ay_r, ax_s, ax_r,
    st, st_y_in, st_x_in, sy_s, sy_r, sx_s, sx_r,
    xo, xi, xo_s, xo_r,
    yo, yi, yo_s, yo_r,
    co, ci, co_s, co_r,
    zo, zi, zo_s, zo_r,
):
    tok = lax.axis_index("tok")
    code = lax.axis_index("code")
    core = lax.rem(code, CORES)
    y = lax.rem(code // CORES, y_n)
    x = code // (CORES * y_n)
    rows = lat_h.shape[0]
    lat_w = wd_h.shape[1]
    codes = cb_h.shape[0]
    block = y_n * rows
    width = 2 * block
    z_parts = zo.shape[2]
    x_parts = xo.shape[2]
    share = codes // z_n
    z_rows = share // z_parts
    mine = core * codes
    other = (1 - core) * codes

    def at_code(x_at, y_at, core_at):
        return {"code": (x_at * y_n + y_at) * CORES + core_at}

    sibling = at_code(x, y, 1 - core)

    def y_peer(step):
        return at_code(x, lax.rem(y + step, y_n), core)

    def x_peer(step):
        return at_code(lax.rem(x + step + x_n, x_n), y, core)

    def z_peer(step):
        return {"tok": lax.rem(tok + step + z_n, z_n)}

    def remote(src, dst, send_sem, recv_sem, device):
        return pltpu.make_async_remote_copy(
            src_ref=src, dst_ref=dst, send_sem=send_sem, recv_sem=recv_sem, device_id=device, device_id_type=MESH
        )

    sent = []

    def push(*args):
        copy = remote(*args)
        copy.start()
        sent.append(copy)

    def drain():
        while sent:
            sent.pop(0).wait_send()

    def pull(dst, recv_sem, device):
        remote(dst, dst, cb_s.at[0], recv_sem, device).wait_recv()

    def span(start, size):
        return pl.ds(pl.multiple_of(start, size), size)

    loads = [
        pltpu.make_async_copy(src, dst, load_sem.at[i])
        for i, (src, dst) in enumerate(
            ((lat_h, lat), (wd_h, wd), (go_h, go), (wu_h, wu), (cb_h, cb.at[span(mine, codes), :]))
        )
    ]
    for load in loads:
        load.start()

    peers = [sibling] + [y_peer(s) for s in range(1, y_n)] + [x_peer(s) for s in range(1, x_n)]
    peers += [z_peer(1), z_peer(-1)]
    barrier = pltpu.get_barrier_semaphore()
    for peer in peers:
        pl.semaphore_signal(barrier, inc=1, device_id=peer, device_id_type=MESH)

    place_of = {j: i for i, j in enumerate((0, x_n - 1, 1, 2))}

    def chunk(j, start, size):
        pair, second = divmod(place_of[j], 2)
        return gat.at[pair, :, span(second * block + start, size), :]

    def lanes(j):
        return pl.ds(place_of[j] % 2 * block, block)

    loads[0].wait()
    loads[1].wait()
    proj = dot_nn(lat[...], wd[...])
    lnorm = jnp.sqrt(jnp.sum(proj * proj, axis=1, keepdims=True) + epsilon)
    unit = proj / lnorm
    own[0] = unit
    own[1] = jnp.broadcast_to(lnorm, unit.shape)
    gat[0, 0, span(y * rows, rows), :] = (unit.astype(BF16).astype(F32) * logit_scale).astype(BF16)
    loads[2].wait()
    loads[3].wait()
    gat[0, 1, span(y * rows, rows), :] = dot_nt(go[...], wu[...]).astype(BF16)

    pl.semaphore_wait(barrier, len(peers))

    near = sorted(range(1, y_n), key=lambda s: min(s, y_n - s))

    def along_x(s):
        from_y = lax.rem(y + y_n - s, y_n) * rows
        for i, step in enumerate((2, 1, -1)):
            slot = -step % x_n
            push(chunk(0, from_y, rows), chunk(slot, from_y, rows), ax_s.at[s, i], ax_r.at[slot - 1], x_peer(step))

    for s in near:
        piece = chunk(0, y * rows, rows)
        push(piece, piece, ay_s.at[s - 1], ay_r.at[s - 1], y_peer(s))
    along_x(0)
    push(cb_h, cb.at[span(mine, codes), :], cb_s.at[0], cb_r.at[0], sibling)

    step_rows = min(256, codes)
    steps = codes // step_rows

    def normalize(i):
        if i == 0:
            loads[4].wait()
        if i == steps:
            pull(cb.at[span(other, codes), :], cb_r.at[0], sibling)
        at = span((mine if i < steps else other) + i % steps * step_rows, step_rows)
        c = cb[at, :].astype(F32)
        n = c / jnp.sqrt(jnp.sum(c * c, axis=1, keepdims=True) + epsilon)
        n = n.astype(BF16)
        low[at, :] = n
        low_t[:, at] = n.T

    todo = list(range(2 * steps))
    for _ in range(min(6, steps)):
        normalize(todo.pop(0))
    for s in near:
        pull(chunk(0, lax.rem(y + y_n - s, y_n) * rows, rows), ay_r.at[s - 1], y_peer(s))
        along_x(s)
        if todo:
            normalize(todo.pop(0))
    for i in todo:
        normalize(i)

    tile = min(512, codes)
    sums = {}

    def forward(pair):
        u = gat[pair, 0]
        g = gat[pair, 1]
        col = pl.ds(pair * width, width)
        col_h = pl.ds((2 + pair) * width, width)

        def step(i, carry):
            den, inn = carry
            at = span(i * tile, tile)
            n = low[at, :]
            e = jnp.exp(dot_nt(n, u))
            eh = e * dot_nt(n, g)
            ee[at, col] = e.astype(BF16)
            ee[at, col_h] = eh.astype(BF16)
            return den + e.reshape(tile // 8, 8, width).sum(0), inn + eh.reshape(tile // 8, 8, width).sum(0)

        zero = jnp.zeros((8, width), F32)
        den, inn = lax.fori_loop(0, CORES * codes // tile, step, (zero, zero), unroll=True)
        sums[pair] = (jnp.sum(den, axis=0, keepdims=True), jnp.sum(inn, axis=0, keepdims=True))
        tr[pair, 0] = u.T
        tr[pair, 1] = g.T

    def weighted(pair):
        na[pair, 0] = dot_nn(low_t[...], ee[:, pl.ds(pair * width, width)]).astype(BF16)
        na[pair, 1] = dot_nn(low_t[...], ee[:, pl.ds((2 + pair) * width, width)]).astype(BF16)

    def from_x(j):
        pull(chunk(j, 0, block), ax_r.at[j - 1], x_peer(j))

    from_x(x_n - 1)
    forward(0)
    from_x(1)
    from_x(2)
    forward(1)

    line = lax.broadcasted_iota(jnp.int32, (2 * x_n, block), 0)
    part = jnp.zeros((2 * x_n, block), F32)
    for j in range(x_n):
        at_x = lax.rem(x + j, x_n)
        first = place_of[j] % 2 * block
        for i in range(2):
            part = jnp.where(line == 2 * at_x + i, sums[place_of[j] // 2][i][:, first : first + block], part)
    st[0] = part
    for s in reversed(near):
        push(st.at[0], st_y_in.at[s - 1], sy_s.at[s - 1], sy_r.at[s - 1], y_peer(s))
    weighted(0)
    weighted(1)
    drain()

    ring_x = RingSum(x_n, xo, xi, xo_s, xo_r, x_peer)

    def token_sum(j, kind):
        return na[place_of[j] // 2, kind, :, lanes(j)].astype(F32)

    def send_x(wanted):
        for sign in (1, -1):
            for k, kind in ring_x.order(sign):
                if wanted(k == longest(x_n, x_parts, sign, kind)):
                    ring_x.send(sign, k, kind, token_sum((sign * k) % x_n, kind))

    send_x(lambda begins: begins)

    for s in near:
        pull(st_y_in.at[s - 1], sy_r.at[s - 1], y_peer(s))
        part = part + st_y_in[s - 1]
    st[1] = part
    for s in range(1, x_n):
        push(st.at[1], st_x_in.at[s - 1], sx_s.at[s - 1], sx_r.at[s - 1], x_peer(s))
    send_x(lambda begins: not begins)
    for s in range(1, x_n):
        pull(st_x_in.at[s - 1], sx_r.at[s - 1], x_peer(s))
        part = part + st_x_in[s - 1]
    total = part

    def line_of(at):
        return jnp.sum(jnp.where(line == at, total, 0.0), axis=0, keepdims=True)

    for pair in range(2):
        at_x = [lax.rem(x + j, x_n) for j in sorted(place_of, key=place_of.get)[2 * pair : 2 * pair + 2]]
        den = jnp.concatenate([line_of(2 * at) for at in at_x], axis=1)
        inner = jnp.concatenate([line_of(2 * at + 1) for at in at_x], axis=1) / den
        inv = 1.0 / den
        ut = tr[pair, 0].astype(F32)
        gt = tr[pair, 1].astype(F32)
        wt[:, pl.ds(pair * width, width)] = ((gt - inner * ut) * inv).astype(BF16)
        wt[:, pl.ds((2 + pair) * width, width)] = (ut * inv).astype(BF16)

    ring_z = RingSum(z_n, zo, zi, zo_s, zo_r, z_peer)
    top = z_n // 2
    steps_z = [top]
    for k in range(top - 1, 0, -1):
        steps_z += [k, z_n - k]
    steps_z.append(0)

    def shard_rows(half, step):
        return span(half + lax.rem(tok + step, z_n) * share, share)

    def give(steps):
        for step in steps:
            co[step] = dot_nt(ee[shard_rows(other, step), :], wt[...]).astype(BF16)
        for step in steps:
            push(co.at[step], ci.at[step], co_s.at[step], co_r.at[step], sibling)

    def shards(steps):
        for step in steps:
            grad[step] = dot_nt(ee[shard_rows(mine, step), :], wt[...])
        for step in steps:
            pull(ci.at[step], co_r.at[step], sibling)
            grad[step] += ci[step].astype(F32)

    def send_z(sign, k, part):
        ring_z.send(sign, k, part, grad[(sign * k) % z_n, pl.ds(part * z_rows, z_rows), :])

    def tokens_y():
        for kind in range(2):
            both = ring_x.total(kind, token_sum(0, kind)).T.astype(BF16)
            yo[:, :, kind * lat_w : (kind + 1) * lat_w] = both.reshape(y_n, rows, lat_w)
        for s in range(1, y_n):
            push(yo.at[lax.rem(y + s, y_n)], yi.at[s - 1], yo_s.at[s - 1], yo_r.at[s - 1], y_peer(s))

    def send_all(wanted):
        order = [[m for m in ring_z.order(sign) if wanted(sign, *m)] for sign in (1, -1)]
        for pair in itertools.zip_longest(*order):
            for sign, message in zip((1, -1), pair):
                if message is not None:
                    send_z(sign, *message)

    def begins(sign, k, part):
        return k == longest(z_n, z_parts, sign, part)

    give(steps_z[:1])
    give(steps_z[1:3])
    shards(steps_z[:1])
    send_all(lambda sign, k, part: k == top and begins(sign, k, part))
    shards(steps_z[1:3])
    send_all(lambda sign, k, part: k < top and begins(sign, k, part))
    give(steps_z[3:])
    shards(steps_z[3:])
    for k in range(top - 1, 0, -1):
        send_all(lambda sign, at, part: at == k and not begins(sign, at, part))
        if k == top - 1:
            tokens_y()
    if top == 1:
        tokens_y()

    sums_own = yo[y].astype(F32)
    for s in near:
        pull(yi.at[s - 1], yo_r.at[s - 1], y_peer(s))
        sums_own = sums_own + yi[s - 1].astype(F32)
    numer = sums_own[:, :lat_w]
    pulled = sums_own[:, lat_w:]
    lane = lax.broadcasted_iota(jnp.int32, (rows, block), 1)
    first = lax.broadcasted_iota(jnp.int32, (rows, block), 0) + y * rows

    def column(at):
        return jnp.sum(jnp.where(lane == first, line_of(at), 0.0), axis=1, keepdims=True)

    den = column(2 * x)
    inner = column(2 * x + 1) / den
    soft = numer / den
    q_out[...] = dot_nn(soft.astype(BF16), wu[...]).astype(BF16)
    grad_unit = (pulled - inner * numer) / den * logit_scale
    unit = own[0]
    grad_proj = (grad_unit - unit * jnp.sum(unit * grad_unit, axis=1, keepdims=True)) / own[1]
    gl_out[...] = dot_nt(grad_proj.astype(BF16), wd[...]).astype(BF16)

    drain()
    ring_z.sent, last = ring_z.sent[-2 * z_parts :], ring_z.sent[: -2 * z_parts]
    for copy in ring_x.sent + last:
        copy.wait_send()

    for part in sorted(range(z_parts), key=lambda p: min(p, z_parts - 1 - p), reverse=True):
        at = pl.ds(part * z_rows, z_rows)
        c = cb[span(mine + tok * share + part * z_rows, z_rows), :].astype(F32)
        cnorm = jnp.sqrt(jnp.sum(c * c, axis=1, keepdims=True) + epsilon)
        n = c / cnorm
        gn = ring_z.total(part, grad[0, at, :])
        gcb_out[at, :] = (gn - n * jnp.sum(n * gn, axis=1, keepdims=True)) / cnorm

    for copy in ring_z.sent:
        copy.wait_send()


def place(*refs):
    n = len(refs) // 2
    copies = [pltpu.make_async_copy(refs[i], refs[n + i], refs[-1].at[i]) for i in range(n)]
    for copy in copies:
        copy.start()
    for copy in copies:
        copy.wait()


def solution(mesh):
    z_n = mesh.shape["tok"]
    x_n = X_CHIPS
    y_n = mesh.shape["code"] // (CORES * x_n)

    def local(latents, w_down, w_up, codebook, grad_out):
        rows, d = latents.shape
        lat_w = w_down.shape[1]
        codes = codebook.shape[0]
        width = 2 * y_n * rows
        sem = lambda *shape: pltpu.SemaphoreType.DMA(shape)
        ring = lambda n, parts, r, w: [
            pltpu.VMEM((2, n // 2, parts, r // parts, w), BF16),
            pltpu.VMEM((2, n // 2, parts, r // parts, w), BF16),
            sem(2, n // 2, parts),
            sem(2, n // 2, parts),
        ]
        any_space = pl.BlockSpec(memory_space=pl.ANY)
        vmem = pl.BlockSpec(memory_space=pltpu.VMEM)
        stats = (2 * x_n, width // 2)
        outs = (
            jax.ShapeDtypeStruct((rows, d), BF16),
            jax.ShapeDtypeStruct((rows, d), BF16),
            jax.ShapeDtypeStruct((codes // z_n, lat_w), F32),
        )
        results = pl.pallas_call(
            functools.partial(kernel, x_n, y_n, z_n),
            out_shape=outs,
            in_specs=[any_space] * 5,
            out_specs=(vmem, vmem, vmem),
            scratch_shapes=[
                pltpu.VMEM(latents.shape, BF16),
                pltpu.VMEM(w_down.shape, BF16),
                pltpu.VMEM(w_up.shape, BF16),
                pltpu.VMEM((CORES * codes, lat_w), BF16),
                pltpu.VMEM(grad_out.shape, BF16),
                sem(5), sem(1), sem(1),
                pltpu.VMEM((2, 2, width, lat_w), BF16),
                pltpu.VMEM((CORES * codes, lat_w), BF16),
                pltpu.VMEM((lat_w, CORES * codes), BF16),
                pltpu.VMEM((CORES * codes, 4 * width), BF16),
                pltpu.VMEM((lat_w, 4 * width), BF16),
                pltpu.VMEM((2, 2, lat_w, width), BF16),
                pltpu.VMEM((2, 2, lat_w, width), BF16),
                pltpu.VMEM((z_n, codes // z_n, lat_w), F32),
                pltpu.VMEM((2, rows, lat_w), F32),
                sem(y_n - 1), sem(y_n - 1), sem(y_n, x_n - 1), sem(x_n - 1),
                pltpu.VMEM((2,) + stats, F32),
                pltpu.VMEM((y_n - 1,) + stats, F32),
                pltpu.VMEM((x_n - 1,) + stats, F32),
                sem(y_n - 1), sem(y_n - 1), sem(x_n - 1), sem(x_n - 1),
                *ring(x_n, 2, 2 * lat_w, width // 2),
                pltpu.VMEM((y_n, rows, 2 * lat_w), BF16),
                pltpu.VMEM((y_n - 1, rows, 2 * lat_w), BF16),
                sem(y_n - 1), sem(y_n - 1),
                pltpu.VMEM((z_n, codes // z_n, lat_w), BF16),
                pltpu.VMEM((z_n, codes // z_n, lat_w), BF16),
                sem(z_n), sem(z_n),
                *ring(z_n, 4, codes // z_n, lat_w),
            ],
            compiler_params=pltpu.CompilerParams(
                collective_id=0, has_side_effects=True, vmem_limit_bytes=64 * 2**20 - 64 * 2**10
            ),
        )(latents, w_down, w_up, codebook, grad_out)
        return pl.pallas_call(
            place,
            out_shape=outs,
            in_specs=[vmem] * 3,
            out_specs=(any_space,) * 3,
            scratch_shapes=[sem(3)],
        )(*results)

    return jax.shard_map(
        local,
        mesh=mesh,
        in_specs=(P(("tok", "code"), None), P(), P(), P("code", None), P(("tok", "code"), None)),
        out_specs=(P(("tok", "code"), None), P(("tok", "code"), None), P(("code", "tok"), None)),
        check_vma=False,
    )
```

time: 58.3 us -> 55.6 us (0.954)
  Pallas kernels: 56.7 us -> 54.2 us
    pallas_call x1, Pallas kernels: 54.9 us -> 52.4 us  [local(): pl.pallas_call(functools.partial(kernel, x_n, y_n, z_n), out_shape=outs,...]
where the time goes in v3:
time: 55.6 us; the launch traced here: 54.8 us
  Pallas kernels  54.2 us (97%)
  between operations  0.64 us (1%)
    pallas_call x1, Pallas kernels, local(): pl.pallas_call(functools.partial(kernel, x_n, y_n, z_n), out_shape=outs,...  52.4 us
    pallas_call x1, Pallas kernels, local(): pl.pallas_call(place, out_shape=outs, in_specs=[vmem] * 3, out_specs=(any...  1.74 us

profile of v3, /device:TPU:1, one launch (start us, length us, event | category | flops | bytes accessed | tf_op | source)
XLA Modules:
  0.0 54.8 jit_solution(2971036512956913078)
XLA Ops:
  0.6 52.4 %shard_map.76 = (bf16[16,1024]{1,0:T(8,128)(2,1)}, bf16[16,1024]{1,0:T(8,128)(2,1)}, f32[256,256]{1,0:T(8,128)}) custom-call(bf16[16,1024]{1,0:T(8,128)(2,1)} %lat_h.1, bf16[1024,256]{1,0:T(8,128)(2,1)} %wd_h.1, bf16[256,1024]{1,0:T(8,128)(2,1)} %wu_h.1, bf16[2048,256]{1,0:T(8,128)(2,1)} %cb_h.1, bf16[16,1024]{1,0:T(8,128)(2,1)} %go_h.1), custom_call_target="tpu_custom_call" | custom-call | tf_op jit(solution)/shard_map/pallas_call | solution.py:441
  53.1 1.7 %shard_map.77 = (bf16[16,1024]{1,0:T(8,128)(2,1)}, bf16[16,1024]{1,0:T(8,128)(2,1)}, f32[256,256]{1,0:T(8,128)}) custom-call(bf16[16,1024]{1,0:T(8,128)(2,1)} %get-tuple-element.6.refs_0_, bf16[16,1024]{1,0:T(8,128)(2,1)} %get-tuple-element.7.refs_1_, f32[256,256]{1,0:T(8,128)} %get-tuple-element.8.refs_2_), custom_call_target="tpu_custom_call" | custom-call | tf_op jit(solution)/shard_map/pallas_call | solution.py:480

commit v4 on v3

--- a/solution.py
+++ b/solution.py
@@ -77,7 +77,7 @@
 def kernel(
     x_n, y_n, z_n,
     lat_h, wd_h, wu_h, cb_h, go_h,
-    q_out, gl_out, gcb_out,
+    q_hbm, gl_hbm, gcb_hbm,
     lat, wd, wu, cb, go, load_sem, cb_s, cb_r,
     gat, low, low_t, ee, wt, tr, na, grad, own,
     ay_s, ay_r, ax_s, ax_r,
@@ -86,6 +86,7 @@
     yo, yi, yo_s, yo_r,
     co, ci, co_s, co_r,
     zo, zi, zo_s, zo_r,
+    q_out, gl_out, gcb_out, fin, out_sem,
 ):
     tok = lax.axis_index("tok")
     code = lax.axis_index("code")
@@ -140,6 +141,12 @@
     def span(start, size):
         return pl.ds(pl.multiple_of(start, size), size)
 
+    peers = [sibling] + [y_peer(s) for s in range(1, y_n)] + [x_peer(s) for s in range(1, x_n)]
+    peers += [z_peer(1), z_peer(-1)]
+    barrier = pltpu.get_barrier_semaphore()
+    for peer in peers:
+        pl.semaphore_signal(barrier, inc=1, device_id=peer, device_id_type=MESH)
+
     loads = [
         pltpu.make_async_copy(src, dst, load_sem.at[i])
         for i, (src, dst) in enumerate(
@@ -149,20 +156,8 @@
     for load in loads:
         load.start()
 
-    peers = [sibling] + [y_peer(s) for s in range(1, y_n)] + [x_peer(s) for s in range(1, x_n)]
-    peers += [z_peer(1), z_peer(-1)]
-    barrier = pltpu.get_barrier_semaphore()
-    for peer in peers:
-        pl.semaphore_signal(barrier, inc=1, device_id=peer, device_id_type=MESH)
-
-    place_of = {j: i for i, j in enumerate((0, x_n - 1, 1, 2))}
-
     def chunk(j, start, size):
-        pair, second = divmod(place_of[j], 2)
-        return gat.at[pair, :, span(second * block + start, size), :]
-
-    def lanes(j):
-        return pl.ds(place_of[j] % 2 * block, block)
+        return gat.at[j, :, span(start, size), :]
 
     loads[0].wait()
     loads[1].wait()
@@ -221,59 +216,55 @@
     tile = min(512, codes)
     sums = {}
 
-    def forward(pair):
-        u = gat[pair, 0]
-        g = gat[pair, 1]
-        col = pl.ds(pair * width, width)
-        col_h = pl.ds((2 + pair) * width, width)
+    def forward(j):
+        both = gat[j].reshape(width, lat_w)
+        col = pl.ds(j * width, block)
+        col_h = pl.ds(j * width + block, block)
 
         def step(i, carry):
             den, inn = carry
             at = span(i * tile, tile)
-            n = low[at, :]
-            e = jnp.exp(dot_nt(n, u))
-            eh = e * dot_nt(n, g)
+            products = dot_nt(low[at, :], both)
+            e = jnp.exp(products[:, :block])
+            eh = e * products[:, block:]
             ee[at, col] = e.astype(BF16)
             ee[at, col_h] = eh.astype(BF16)
-            return den + e.reshape(tile // 8, 8, width).sum(0), inn + eh.reshape(tile // 8, 8, width).sum(0)
-
-        zero = jnp.zeros((8, width), F32)
+            return den + e.reshape(tile // 8, 8, block).sum(0), inn + eh.reshape(tile // 8, 8, block).sum(0)
+
+        zero = jnp.zeros((8, block), F32)
         den, inn = lax.fori_loop(0, CORES * codes // tile, step, (zero, zero), unroll=True)
-        sums[pair] = (jnp.sum(den, axis=0, keepdims=True), jnp.sum(inn, axis=0, keepdims=True))
-        tr[pair, 0] = u.T
-        tr[pair, 1] = g.T
-
-    def weighted(pair):
-        na[pair, 0] = dot_nn(low_t[...], ee[:, pl.ds(pair * width, width)]).astype(BF16)
-        na[pair, 1] = dot_nn(low_t[...], ee[:, pl.ds((2 + pair) * width, width)]).astype(BF16)
+        sums[j] = (jnp.sum(den, axis=0, keepdims=True), jnp.sum(inn, axis=0, keepdims=True))
+        tr[j] = both.T
+
+    def weighted(j):
+        na[j] = dot_nn(low_t[...], ee[:, pl.ds(j * width, width)]).astype(BF16)
 
     def from_x(j):
         pull(chunk(j, 0, block), ax_r.at[j - 1], x_peer(j))
 
-    from_x(x_n - 1)
     forward(0)
-    from_x(1)
-    from_x(2)
-    forward(1)
+    arriving = (x_n - 1, 1, 2)
+    for j in arriving:
+        from_x(j)
+        forward(j)
 
     line = lax.broadcasted_iota(jnp.int32, (2 * x_n, block), 0)
     part = jnp.zeros((2 * x_n, block), F32)
     for j in range(x_n):
         at_x = lax.rem(x + j, x_n)
-        first = place_of[j] % 2 * block
         for i in range(2):
-            part = jnp.where(line == 2 * at_x + i, sums[place_of[j] // 2][i][:, first : first + block], part)
+            part = jnp.where(line == 2 * at_x + i, sums[j][i], part)
     st[0] = part
     for s in reversed(near):
         push(st.at[0], st_y_in.at[s - 1], sy_s.at[s - 1], sy_r.at[s - 1], y_peer(s))
-    weighted(0)
-    weighted(1)
+    for j in (0,) + arriving:
+        weighted(j)
     drain()
 
     ring_x = RingSum(x_n, xo, xi, xo_s, xo_r, x_peer)
 
     def token_sum(j, kind):
-        return na[place_of[j] // 2, kind, :, lanes(j)].astype(F32)
+        return na[j, :, pl.ds(kind * block, block)].astype(F32)
 
     def send_x(wanted):
         for sign in (1, -1):
@@ -298,15 +289,15 @@
     def line_of(at):
         return jnp.sum(jnp.where(line == at, total, 0.0), axis=0, keepdims=True)
 
-    for pair in range(2):
-        at_x = [lax.rem(x + j, x_n) for j in sorted(place_of, key=place_of.get)[2 * pair : 2 * pair + 2]]
-        den = jnp.concatenate([line_of(2 * at) for at in at_x], axis=1)
-        inner = jnp.concatenate([line_of(2 * at + 1) for at in at_x], axis=1) / den
+    for j in range(x_n):
+        at_x = lax.rem(x + j, x_n)
+        den = line_of(2 * at_x)
+        inner = line_of(2 * at_x + 1) / den
         inv = 1.0 / den
-        ut = tr[pair, 0].astype(F32)
-        gt = tr[pair, 1].astype(F32)
-        wt[:, pl.ds(pair * width, width)] = ((gt - inner * ut) * inv).astype(BF16)
-        wt[:, pl.ds((2 + pair) * width, width)] = (ut * inv).astype(BF16)
+        ut = tr[j, :, :block].astype(F32)
+        gt = tr[j, :, block:].astype(F32)
+        wt[:, pl.ds(j * width, block)] = ((gt - inner * ut) * inv).astype(BF16)
+        wt[:, pl.ds(j * width + block, block)] = (ut * inv).astype(BF16)
 
     ring_z = RingSum(z_n, zo, zi, zo_s, zo_r, z_peer)
     top = z_n // 2
@@ -358,13 +349,19 @@
     shards(steps_z[1:3])
     send_all(lambda sign, k, part: k < top and begins(sign, k, part))
     give(steps_z[3:])
-    shards(steps_z[3:])
+    shards(steps_z[3:5])
+    tokens_y()
     for k in range(top - 1, 0, -1):
-        send_all(lambda sign, at, part: at == k and not begins(sign, at, part))
-        if k == top - 1:
-            tokens_y()
-    if top == 1:
-        tokens_y()
+        for top_at in (top - 1, top):
+            send_all(
+                lambda sign, at, part: at == k
+                and longest(z_n, z_parts, sign, part) == top_at
+                and not begins(sign, at, part)
+            )
+            if k == top - 2 and top_at == top - 1:
+                shards(steps_z[5:])
+    if top < 3:
+        shards(steps_z[5:])
 
     sums_own = yo[y].astype(F32)
     for s in near:
@@ -386,20 +383,33 @@
     unit = own[0]
     grad_proj = (grad_unit - unit * jnp.sum(unit * grad_unit, axis=1, keepdims=True)) / own[1]
     gl_out[...] = dot_nt(grad_proj.astype(BF16), wd[...]).astype(BF16)
+    outs = [
+        pltpu.make_async_copy(q_out, q_hbm, out_sem.at[0]),
+        pltpu.make_async_copy(gl_out, gl_hbm, out_sem.at[1]),
+    ]
+    for copy in outs:
+        copy.start()
 
     drain()
     ring_z.sent, last = ring_z.sent[-2 * z_parts :], ring_z.sent[: -2 * z_parts]
     for copy in ring_x.sent + last:
         copy.wait_send()
 
-    for part in sorted(range(z_parts), key=lambda p: min(p, z_parts - 1 - p), reverse=True):
+    c = cb[span(mine + tok * share, share), :].astype(F32)
+    inv = 1.0 / jnp.sqrt(jnp.sum(c * c, axis=1, keepdims=True) + epsilon)
+    fin[0] = c * inv
+    fin[1] = jnp.broadcast_to(inv, c.shape)
+    for part in sorted(range(z_parts), key=lambda p: (p % (z_parts // 2), p)):
         at = pl.ds(part * z_rows, z_rows)
-        c = cb[span(mine + tok * share + part * z_rows, z_rows), :].astype(F32)
-        cnorm = jnp.sqrt(jnp.sum(c * c, axis=1, keepdims=True) + epsilon)
-        n = c / cnorm
+        n = fin[0, at, :]
         gn = ring_z.total(part, grad[0, at, :])
-        gcb_out[at, :] = (gn - n * jnp.sum(n * gn, axis=1, keepdims=True)) / cnorm
-
+        gcb_out[at, :] = (gn - n * jnp.sum(n * gn, axis=1, keepdims=True)) * fin[1, at, :]
+        copy = pltpu.make_async_copy(gcb_out.at[at, :], gcb_hbm.at[at, :], out_sem.at[2 + part])
+        copy.start()
+        outs.append(copy)
+
+    for copy in outs:
+        copy.wait()
     for copy in ring_z.sent:
         copy.wait_send()
 
@@ -442,7 +452,7 @@
             functools.partial(kernel, x_n, y_n, z_n),
             out_shape=outs,
             in_specs=[any_space] * 5,
-            out_specs=(vmem, vmem, vmem),
+            out_specs=(any_space,) * 3,
             scratch_shapes=[
                 pltpu.VMEM(latents.shape, BF16),
                 pltpu.VMEM(w_down.shape, BF16),
@@ -450,13 +460,13 @@
                 pltpu.VMEM((CORES * codes, lat_w), BF16),
                 pltpu.VMEM(grad_out.shape, BF16),
                 sem(5), sem(1), sem(1),
-                pltpu.VMEM((2, 2, width, lat_w), BF16),
+                pltpu.VMEM((x_n, 2, width // 2, lat_w), BF16),
                 pltpu.VMEM((CORES * codes, lat_w), BF16),
                 pltpu.VMEM((lat_w, CORES * codes), BF16),
-                pltpu.VMEM((CORES * codes, 4 * width), BF16),
-                pltpu.VMEM((lat_w, 4 * width), BF16),
-                pltpu.VMEM((2, 2, lat_w, width), BF16),
-                pltpu.VMEM((2, 2, lat_w, width), BF16),
+                pltpu.VMEM((CORES * codes, x_n * width), BF16),
+                pltpu.VMEM((lat_w, x_n * width), BF16),
+                pltpu.VMEM((x_n, lat_w, width), BF16),
+                pltpu.VMEM((x_n, lat_w, width), BF16),
                 pltpu.VMEM((z_n, codes // z_n, lat_w), F32),
                 pltpu.VMEM((2, rows, lat_w), F32),
                 sem(y_n - 1), sem(y_n - 1), sem(y_n, x_n - 1), sem(x_n - 1),
@@ -472,6 +482,11 @@
                 pltpu.VMEM((z_n, codes // z_n, lat_w), BF16),
                 sem(z_n), sem(z_n),
                 *ring(z_n, 4, codes // z_n, lat_w),
+                pltpu.VMEM((rows, d), BF16),
+                pltpu.VMEM((rows, d), BF16),
+                pltpu.VMEM((codes // z_n, lat_w), F32),
+                pltpu.VMEM((2, codes // z_n, lat_w), F32),
+                sem(2 + 4),
             ],
             compiler_params=pltpu.CompilerParams(
                 collective_id=0, has_side_effects=True, vmem_limit_bytes=64 * 2**20 - 64 * 2**10

time: 55.6 us -> 54.7 us (0.984)
  Pallas kernels: 54.2 us -> 53.5 us
    pallas_call x1, Pallas kernels: 52.4 us -> 51.7 us  [local(): pl.pallas_call(functools.partial(kernel, x_n, y_n, z_n), out_shape=outs,...]
where the time goes in v4:
time: 54.7 us; the launch traced here: 54.1 us
  Pallas kernels  53.5 us (98%)
  between operations  0.64 us (1%)
    pallas_call x1, Pallas kernels, local(): pl.pallas_call(functools.partial(kernel, x_n, y_n, z_n), out_shape=outs,...  51.7 us
    pallas_call x1, Pallas kernels, local(): pl.pallas_call(place, out_shape=outs, in_specs=[vmem] * 3, out_specs=(any...  1.74 us

profile of v4, /device:TPU:1, one launch (start us, length us, event | category | flops | bytes accessed | tf_op | source)
XLA Modules:
  0.0 54.1 jit_solution(12768716226118499945)
XLA Ops:
  0.6 51.7 %shard_map.76 = (bf16[16,1024]{1,0:T(8,128)(2,1)}, bf16[16,1024]{1,0:T(8,128)(2,1)}, f32[256,256]{1,0:T(8,128)}) custom-call(bf16[16,1024]{1,0:T(8,128)(2,1)} %lat_h.1, bf16[1024,256]{1,0:T(8,128)(2,1)} %wd_h.1, bf16[256,1024]{1,0:T(8,128)(2,1)} %wu_h.1, bf16[2048,256]{1,0:T(8,128)(2,1)} %cb_h.1, bf16[16,1024]{1,0:T(8,128)(2,1)} %go_h.1), custom_call_target="tpu_custom_call" | custom-call | tf_op jit(solution)/shard_map/pallas_call | solution.py:451
  52.4 1.7 %shard_map.77 = (bf16[16,1024]{1,0:T(8,128)(2,1)}, bf16[16,1024]{1,0:T(8,128)(2,1)}, f32[256,256]{1,0:T(8,128)}) custom-call(bf16[16,1024]{1,0:T(8,128)(2,1)} %get-tuple-element.6.refs_0_, bf16[16,1024]{1,0:T(8,128)(2,1)} %get-tuple-element.7.refs_1_, f32[256,256]{1,0:T(8,128)} %get-tuple-element.8.refs_2_), custom_call_target="tpu_custom_call" | custom-call | tf_op jit(solution)/shard_map/pallas_call | solution.py:495
